TPU v7x, 128 devices: a whole 4x4x4 slice. The times are simulated.
128 devices in a mesh: dp: 8 (over x, y_lo), tensor: 16 (over y_hi, z, core).
Axes of the slice: x: 4, y: 4 (y_hi: 2, y_lo: 2; y = y_hi * 2 + y_lo), z: 4, core: 2. Of those that a mesh axis runs over, the one named last changes fastest.
Arguments:
- gate_pre: bfloat16 [4096, 14848], P('dp', 'tensor'), may hold values from -6 to 6
- up_pre: bfloat16 [4096, 14848], P('dp', 'tensor'), may hold values from -6 to 6
- w_down: bfloat16 [14848, 8192], P('tensor', 'dp'), may hold values from -0.0625 to 0.0625
- cotangent: bfloat16 [4096, 8192], P('dp', 'tensor'), may hold values from -6 to 6
Outputs:
- layer_out: bfloat16 [4096, 8192], P('dp', 'tensor')
- grad_gate: bfloat16 [4096, 14848], P('dp', 'tensor')
- grad_up: bfloat16 [4096, 14848], P('dp', 'tensor')
- grad_down: bfloat16 [14848, 8192], P('tensor', 'dp')
All inputs are finite; a program needn't handle non-finite values.
Results may differ from a plain program's by a relative error of at most 0.018.
Values may be sent and summed in bfloat16 or wider, within the bound.
A program may use at most 128 MiB of HBM per device.

v0:
```python
import jax
import jax.numpy as jnp
from jax import lax
from jax.sharding import PartitionSpec as P


def shards(gate_pre, up_pre, w_down, cotangent):
    gate_val = gate_pre.astype(jnp.float32)
    up_val = up_pre.astype(jnp.float32)
    squash = jax.nn.sigmoid(gate_val)
    hidden = (gate_val * squash * up_val).astype(jnp.bfloat16)
    full_weight = lax.all_gather(w_down, "dp", axis=1, tiled=True)
    partials = jnp.dot(hidden, full_weight, preferred_element_type=jnp.float32)
    layer_out = lax.psum_scatter(
        partials.astype(jnp.bfloat16), "tensor", scatter_dimension=1, tiled=True
    )
    full_cot = lax.all_gather(cotangent, "tensor", axis=1, tiled=True)
    grad_hidden = lax.dot_general(
        full_cot, full_weight, (((1,), (1,)), ((), ())), preferred_element_type=jnp.float32
    )
    grad_up = (grad_hidden * gate_val * squash).astype(jnp.bfloat16)
    grad_gate = (grad_hidden * up_val * squash * (1.0 + gate_val * (1.0 - squash))).astype(
        jnp.bfloat16
    )
    reduced = lax.psum_scatter(
        lax.dot_general(
            full_cot, hidden, (((0,), (0,)), ((), ())), preferred_element_type=jnp.float32
        ).astype(jnp.bfloat16),
        "dp",
        scatter_dimension=0,
        tiled=True,
    ).astype(jnp.float32)
    grad_down = reduced.T.astype(jnp.bfloat16)
    return (layer_out, grad_gate, grad_up, grad_down)


def solution(mesh):
    placed = (P("dp", "tensor"), P("dp", "tensor"), P("tensor", "dp"), P("dp", "tensor"))
    return jax.shard_map(
        shards,
        mesh=mesh,
        in_specs=placed,
        out_specs=(P("dp", "tensor"), P("dp", "tensor"), P("dp", "tensor"), P("tensor", "dp")),
        check_vma=False,
    )
```

profile of v0, /device:TPU:1, one launch (start us, length us, event | category | flops | bytes accessed | tf_op | source)
XLA Modules:
  0.0 800.0 jit_solution(1831811989441199998)
XLA Ops:
  7.2 0.0 copy-start
  7.2 0.0 copy-start.1
  7.2 0.0 all-gather.3.cloned.1.call-start
  7.2 0.7 all-gather.3.cloned.1.call-update
  7.9 0.0 all-gather.5.cloned.1.call-start
  8.0 0.7 all-gather.5.cloned.1.call-update
  8.7 0.0 reduce-scatter.3.cloned.1.call-start
  8.7 300.4 %all-gather.3.cloned.1.call-done = bf16[928,8192]{1,0:T(8,128)(2,1)} async-done(((bf16[928,1024]{1,0:T(8,128)(2,1)}), bf16[928,8192]{1,0:T(8,128)(2,1)}) %all-gather.3.cloned.1.call-update) | async-done | bytes 15204368 | tf_op jit(solution)/shard_map/all_gather | solution.py:12
  309.1 0.0 copy-done
  309.1 0.0 copy-done.1
  309.1 16.8 %convolution_convert_fusion = bf16[512,8192]{1,0:T(8,128)(2,1)} fusion(bf16[928,8192]{1,0:T(8,128)(2,1)} %all-gather.3.cloned.1.call-done, bf16[512,928]{0,1:T(8,128)(2,1)S(1)} %copy-done, bf16[512,928]{0,1:T(8,128)(2,1)S(1)} %copy-done.1), kind=kOutput, calls=%fused_computation.1 | convolution fusion | flops 7792623616 | bytes 25493504 | tf_op jit(solution)/shard_map/dot_general | solution.py:13
  325.9 0.0 reduce-scatter.3.cloned.1.call-update
  325.9 0.0 reduce-scatter.5.cloned.1.call-start
  325.9 64.1 %all-gather.5.cloned.1.call-done = bf16[512,8192]{1,0:T(8,128)(2,1)} async-done(((bf16[512,512]{1,0:T(8,128)(2,1)}), bf16[512,8192]{1,0:T(8,128)(2,1)}) %all-gather.5.cloned.1.call-update) | async-done | bytes 8388624 | tf_op jit(solution)/shard_map/all_gather | solution.py:17
  390.0 15.2 %convert_bitcast_fusion = bf16[8192,928]{0,1:T(8,128)(2,1)} fusion(bf16[512,8192]{1,0:T(8,128)(2,1)} %all-gather.5.cloned.1.call-done, bf16[512,928]{0,1:T(8,128)(2,1)S(1)} %copy-done, bf16[512,928]{0,1:T(8,128)(2,1)S(1)} %copy-done.1), kind=kOutput, calls=%fused_computation | convolution fusion | flops 7796031488 | bytes 25493504 | tf_op jit(solution)/shard_map/dot_general | solution.py:26
  405.3 0.0 reduce-scatter.5.cloned.1.call-update
  405.3 16.8 %fusion.9 = (bf16[512,928]{0,1:T(8,128)(2,1)}, bf16[512,928]{0,1:T(8,128)(2,1)}) fusion(bf16[512,928]{0,1:T(8,128)(2,1)S(1)} %copy-done.1, bf16[512,928]{0,1:T(8,128)(2,1)S(1)} %copy-done, bf16[512,8192]{1,0:T(8,128)(2,1)} %all-gather.5.cloned.1.call-done, bf16[928,8192]{1,0:T(8,128)(2,1)} %all-gather.3.cloned.1.call-done), kind=kOutput, calls=%fused_computation.17 | convolution fusion | flops 7791755264 | bytes 27394048 | tf_op jit(solution)/shard_map/dot_general | solution.py:18
  422.1 71.3 %reduce-scatter.3.cloned.1.call-done = bf16[512,512]{1,0:T(8,128)(2,1)} async-done(((bf16[512,8192]{1,0:T(8,128)(2,1)}), bf16[512,512]{1,0:T(8,128)(2,1)}) %reduce-scatter.3.cloned.1.call-update) | async-done | bytes 524304 | tf_op jit(solution)/shard_map/reduce_scatter | solution.py:14
  493.4 300.1 %reduce-scatter.5.cloned.1.call-done = bf16[1024,928]{0,1:T(8,128)(2,1)} async-done(((bf16[8192,928]{0,1:T(8,128)(2,1)}), bf16[1024,928]{0,1:T(8,128)(2,1)}) %reduce-scatter.5.cloned.1.call-update) | async-done | bytes 1900560 | tf_op jit(solution)/shard_map/reduce_scatter | solution.py:25
Async XLA Ops:
  7.2 301.9 %copy-start = (bf16[512,928]{0,1:T(8,128)(2,1)S(1)}, bf16[512,928]{0,1:T(8,128)(2,1)}, u32[]{:S(2)}) copy-start(bf16[512,928]{0,1:T(8,128)(2,1)} %param.5) | copy-start | bytes 2850820
  7.2 301.9 %copy-start.1 = (bf16[512,928]{0,1:T(8,128)(2,1)S(1)}, bf16[512,928]{0,1:T(8,128)(2,1)}, u32[]{:S(2)}) copy-start(bf16[512,928]{0,1:T(8,128)(2,1)} %param.4) | copy-start | bytes 2850820
  7.2 301.9 %all-gather.3.cloned.1.call-start = ((), (), s32[]{:S(2)}) async-start(), calls=%async_computation.2 | async-start | bytes 17104896 | tf_op jit(solution)/shard_map/all_gather | solution.py:12
  7.9 382.1 %all-gather.5.cloned.1.call-start = ((), (), s32[]{:S(2)}) async-start(), calls=%async_computation.4 | async-start | bytes 8912896 | tf_op jit(solution)/shard_map/all_gather | solution.py:17
  8.7 484.7 %reduce-scatter.3.cloned.1.call-start = ((), (), s32[]{:S(2)}) async-start(), calls=%async_computation.3 | async-start | bytes 8912896 | tf_op jit(solution)/shard_map/reduce_scatter | solution.py:14
  325.9 467.6 %reduce-scatter.5.cloned.1.call-start = ((), (), s32[]{:S(2)}) async-start(), calls=%async_computation.5 | async-start | bytes 17104896 | tf_op jit(solution)/shard_map/reduce_scatter | solution.py:25
Sparse Core Ops, SparseCore 0:
  9.7 299.3 all-gather.2
  311.4 78.6 all-gather.4
  394.9 98.4 reduce-scatter.2
  496.2 297.1 reduce-scatter.4
where the time goes:
time: 800 us
  waiting for transfers between devices  737 us (92%)
  matrix products  48.8 us (6%)
  between operations  13.8 us (2%)
    all_gather x1, waiting for transfers between devices, shards(): full_weight = lax.all_gather(w_down, 'dp', axis=1, tiled=True)  300 us
    reduce_scatter x1, waiting for transfers between devices, shards(): lax.psum_scatter(lax.dot_general(full_cot, hidden, (((0,), (0,)), ((), ()...  300 us
    reduce_scatter x1, waiting for transfers between devices, shards(): lax.psum_scatter(partials.astype(jnp.bfloat16), 'tensor', scatter_dimensi...  71.3 us
    all_gather x1, waiting for transfers between devices, shards(): full_cot = lax.all_gather(cotangent, 'tensor', axis=1, tiled=True)  64.1 us
    dot_general x1, matrix products, shards(): lax.dot_general(full_cot, full_weight, (((1,), (1,)), ((), ())), preferre...  16.8 us
    dot_general x1, matrix products, shards(): partials = jnp.dot(hidden, full_weight, preferred_element_type=jnp.float32)  16.8 us
  transfers between devices with their start and end apart: 4, of which 4 were waited for; matrix products, arithmetic and copies ran while one was open for 6% of the time, Pallas kernels for 0%

commit v1 on v0

v1 whole, which is shorter than its diff:
```python
import jax
import jax.numpy as jnp
from jax import lax
from jax.experimental import pallas as pl
from jax.experimental.pallas import tpu as pltpu
from jax.sharding import PartitionSpec as P

MESH = pl.DeviceIdType.MESH
BF = jnp.bfloat16
F32 = jnp.float32

TOK = 512
FF = 928
DM = 1024
HALF = 512
CUT = 464
C = 2
RC = HALF // C
HC = RC // 2


class Copies:
    def __init__(self, send, recv):
        self.send, self.recv, self.all, self.n = send, recv, [], 0

    def put(self, src, dst, target, landing=None):
        k = self.n
        self.n += 1
        copy = pltpu.make_async_remote_copy(
            src, dst, self.send.at[k], self.recv.at[k], device_id=target, device_id_type=MESH
        )
        copy.start()
        self.all.append((None, copy))
        if landing is None:
            return copy
        return pltpu.make_async_remote_copy(
            src, landing, self.send.at[k], self.recv.at[k], device_id=target, device_id_type=MESH
        )

    def put_or_keep(self, keep, src, dst, target, landing):
        k = self.n
        self.n += 1
        copy = pltpu.make_async_remote_copy(
            src, dst, self.send.at[k], self.recv.at[k], device_id=target, device_id_type=MESH
        )
        own = pltpu.make_async_copy(src, dst, self.recv.at[k])
        pl.when(keep)(own.start)
        pl.when(jnp.logical_not(keep))(copy.start)
        self.all.append((keep, copy))
        got = pltpu.make_async_remote_copy(
            src, landing, self.send.at[k], self.recv.at[k], device_id=target, device_id_type=MESH
        )

        def wait():
            pl.when(keep)(own.wait)
            pl.when(jnp.logical_not(keep))(got.wait_recv)

        return wait

    def finish(self):
        for keep, copy in self.all:
            if keep is None:
                copy.wait_send()
            else:
                pl.when(jnp.logical_not(keep))(copy.wait_send)


def nn(a, b):
    return lax.dot_general(a, b, (((1,), (0,)), ((), ())), preferred_element_type=F32)


def nt(a, b):
    return lax.dot_general(a, b, (((1,), (1,)), ((), ())), preferred_element_type=F32)


def kernel(
    gate, up, w, cot, lay_out, gg_out, gu_out, gd_out,
    HT, CT, WT, OWN, ZM, G, R1, R3, RAB, RO, LO, LS, LX, LH, LD, LY, FIN, SWP,
    acc, gd_stage, lay_stage, gg_stage, gu_stage, send_sem, recv_sem, out_sem,
):
    dp, t = lax.axis_index("dp"), lax.axis_index("tensor")
    x, yl = dp // 2, dp % 2
    yh, z, c = t // 8, (t // 2) % 4, t % 2
    j = t // 2

    def X(d):
        return (((x + d + 4) % 4) * 2 + yl, t)

    def Z(d):
        return (dp, yh * 8 + ((z + d + 4) % 4) * 2 + c)

    YL = (x * 2 + 1 - yl, t)
    YH = (dp, (1 - yh) * 8 + z * 2 + c)
    CORE = (dp, t + 1 - 2 * c)
    T1, T1S = Z(x), Z(4 - x)
    zs = (z - x + 4) % 4
    T2 = ((2 * yh + zs // 2) * 2 + zs % 2, ((yl + yh + zs) % 2) * 8 + z * 2 + c)
    zo = 2 * (x % 2) + yl
    xs, yls = (z - zo + 4) % 4, (yh + x // 2 + yl) % 2
    T2S = (xs * 2 + yls, (x // 2) * 8 + z * 2 + c)
    q = xs * 2 + yls
    SW = (q, 2 * dp + c)
    xi, yli = j // 2, j % 2
    zi = 2 * (xi % 2) + yli
    SWS = (j, ((yl + xi // 2 + yli) % 2) * 8 + ((x + zi) % 4) * 2 + c)
    t1_keep = x == 0
    t2_keep = jnp.logical_and(T2[0] == dp, T2[1] == t)
    sw_keep = jnp.logical_and(SW[0] == dp, SW[1] == t)

    def tok(dx, other):
        row = 1 - yl if other else yl
        return ((x + dx + 4) % 4) * 2 + row

    def slot(g):
        return ((g % 2 + x // 2 + yl) % 2) * 4 + (g // 2 + zo) % 4

    def place(dz, other):
        row = 1 - yh if other else yh
        return row * 4 + (z + dz + 4) % 4

    barrier = pltpu.get_barrier_semaphore()
    greeted = (X(1), X(-1), YL, Z(1), Z(-1), YH, CORE, T1, T1S, T2, T2S, SW, SWS)
    for other in greeted:
        pl.semaphore_signal(barrier, inc=1, device_id=other, device_id_type=MESH)

    for r in range(0, HALF, 128):
        OWN[:, r : r + 128] = cot[r : r + 128, :].astype(F32).T.astype(BF)

    def make_hidden(k, _):
        rows = pl.ds(pl.multiple_of(k * 128, 128), 128)
        g = gate[rows, :].astype(F32)
        h = g * jax.nn.sigmoid(g) * up[rows, :].astype(F32)
        HT[dp, :, rows] = h.T.astype(BF)
        return 0

    lax.fori_loop(0, 4, make_hidden, 0)

    pl.semaphore_wait(barrier, len(greeted))
    cp = Copies(send_sem, recv_sem)

    def piece(ref, *at, k):
        return ref.at[(*at, pl.ds(k * RC, RC))]

    def crow(k, size=RC):
        return pl.ds(pl.multiple_of(c * HALF + k, 16), size)

    t1 = [cp.put_or_keep(t1_keep, OWN.at[pl.ds(k * RC, RC)], ZM.at[pl.ds(k * RC, RC)], T1, ZM.at[pl.ds(k * RC, RC)]) for k in range(C)]
    own = HT.at[dp]
    s1y = cp.put(own, own, YL, HT.at[tok(0, True)])
    s1p = cp.put(own, own, X(1), HT.at[tok(-1, False)])
    s1m = cp.put(own, own, X(-1), HT.at[tok(1, False)])

    for r in range(0, FF, 464):
        WT[:, r : r + 464] = w[r : r + 464, :].astype(F32).T.astype(BF)

    t2_place = (T2[1] // 2)
    t2 = []
    for k in range(C):
        t1[k]()
        t2.append(cp.put_or_keep(t2_keep, ZM.at[pl.ds(k * RC, RC)], CT.at[t2_place, crow(k * RC)], T2, CT.at[j, crow(k * RC)]))

    def make_layer(g):
        s = slot(g)

        def part(k, _):
            cols = pl.ds(pl.multiple_of(k * 256, 256), 256)
            here = pl.ds(pl.multiple_of(c * HALF, HALF), HALF)
            there = pl.ds(pl.multiple_of((1 - c) * HALF, HALF), HALF)
            h = HT[g, :, cols]
            LS[s, :, cols] = nn(WT[there, :], h).astype(BF)
            LO[s, :, cols] = nn(WT[here, :], h).astype(BF)
            return 0

        lax.fori_loop(0, 2, part, 0)
        return cp.put(LS.at[s], LX.at[s], CORE)

    lx = [make_layer(dp)]

    def spread(block, k):
        ref = CT.at[block, crow(k * RC)]
        return cp.put(ref, ref, Z(1)), cp.put(ref, ref, Z(-1))

    def forward(row, k):
        a = CT.at[place(-1, row), crow(k * RC, HC)]
        b = CT.at[place(1, row), crow(k * RC + HC, HC)]
        return cp.put(a, a, Z(1)), cp.put(b, b, Z(-1))

    t3, near_own, near_par = [], [], []
    for k in range(C):
        t2[k]()
        ref = CT.at[j, crow(k * RC)]
        t3.append(cp.put(ref, ref, YH))
        near_own.append(spread(j, k))
    t5 = []

    def cross(block):
        ref = CT.at[block, crow(0, HALF)]
        t5.append(cp.put(ref, ref, CORE))

    cross(j)

    s1p.wait_recv()
    a = HT.at[tok(-1, False), pl.ds(0, CUT)]
    s2a = cp.put(a, a, X(1))
    s1m.wait_recv()
    b = HT.at[tok(1, False), pl.ds(CUT, FF - CUT)]
    s2b = cp.put(b, b, X(-1))
    s1y.wait_recv()
    par = HT.at[tok(0, True)]
    s3p = cp.put(par, par, X(1))
    s3m = cp.put(par, par, X(-1))

    for k in range(C):
        t3[k].wait_recv()
        near_par.append(spread(place(0, True), k))
    cross(place(0, True))

    lx.append(make_layer(tok(0, True)))
    lx.append(make_layer(tok(1, False)))
    lx.append(make_layer(tok(-1, False)))

    far = []
    for row, near in ((False, near_own), (True, near_par)):
        for k in range(C):
            near[k][0].wait_recv()
            near[k][1].wait_recv()
            far.extend(forward(row, k))
        cross(place(1, row))
        cross(place(-1, row))

    s2a.wait_recv()
    s2b.wait_recv()
    two = HT.at[tok(2, False)]
    s4 = cp.put(two, two, YL)
    lx.append(make_layer(tok(2, False)))

    for f in far[: 2 * C]:
        f.wait_recv()
    cross(place(2, False))
    for f in far[2 * C :]:
        f.wait_recv()
    cross(place(2, True))
    s3p.wait_recv()
    s3m.wait_recv()
    lx.append(make_layer(tok(1, True)))
    lx.append(make_layer(tok(-1, True)))
    for f in t5:
        f.wait_recv()

    def make_grad(g):
        s = slot(g)

        def part(k, _):
            cols = pl.ds(pl.multiple_of(k * 256, 256), 256)
            G[g, :, cols] = nn(w[...], CT[s, :, cols]).astype(BF)
            return 0

        lax.fori_loop(0, 2, part, 0)

    make_grad(tok(1, True))
    g3p = cp.put(G.at[tok(1, True)], R3.at[0], X(1))
    make_grad(tok(-1, True))
    g3m = cp.put(G.at[tok(-1, True)], R3.at[1], X(-1))
    make_grad(tok(2, True))
    g1 = cp.put(G.at[tok(2, True)], R1, YL)
    s4.wait_recv()
    lx.append(make_layer(tok(2, True)))

    for f in lx:
        f.wait_recv()

    def pair(block):
        LO[block] = (LO[block].astype(F32) + LX[block].astype(F32)).astype(BF)

    halves, directs = {}, {}
    for n, row in enumerate((True, False)):
        two = place(2, row)
        pair(two)
        for k in range(C):
            halves[n, k] = (
                cp.put(LO.at[two, pl.ds(k * RC, HC)], LH.at[n, 0, k], Z(1)),
                cp.put(LO.at[two, pl.ds(k * RC + HC, HC)], LH.at[n, 1, k], Z(-1)),
            )
        pair(place(1, row))
        pair(place(-1, row))
    for dx in (2, 1, -1):
        make_grad(tok(dx, False))
    for n, row in enumerate((True, False)):
        for k in range(C):
            sent = []
            for side, dz in ((0, 1), (1, -1)):
                block = place(dz, row)
                halves[n, k][side].wait_recv()
                at = pl.ds(k * RC + side * HC, HC)
                LO[block, at] = (LO[block, at].astype(F32) + LH[n, side, k].astype(F32)).astype(BF)
                at = pl.ds(k * RC, RC)
                sent.append(cp.put(LO.at[block, at], LD.at[n, side, at], Z(dz)))
            directs[n, k] = sent
    pair(place(0, True))
    make_grad(tok(0, True))

    g1.wait_recv()
    two = tok(2, False)
    G[two] = (G[two].astype(F32) + R1[...].astype(F32)).astype(BF)
    g2a = cp.put(G.at[two, pl.ds(0, CUT)], RAB.at[pl.ds(0, CUT)], X(1))
    g2b = cp.put(G.at[two, pl.ds(CUT, FF - CUT)], RAB.at[pl.ds(CUT, FF - CUT)], X(-1))
    make_grad(dp)

    def weight_grad(n):
        cols = pl.ds(n * 256, 256)
        acc[...] = jnp.zeros_like(acc)

        def add(g, _):
            acc[...] += nt(HT[g], CT[slot(g), cols, :])
            return 0

        lax.fori_loop(0, 8, add, 0)
        gd_stage[n % 2] = acc[...].astype(BF)
        copy = pltpu.make_async_copy(gd_stage.at[n % 2], gd_out.at[:, cols], out_sem.at[n])
        copy.start()
        return copy

    outs = [weight_grad(0)]

    g3p.wait_recv()
    g3m.wait_recv()
    par = tok(0, True)
    G[par] = (G[par].astype(F32) + R3[0].astype(F32) + R3[1].astype(F32)).astype(BF)
    g4 = cp.put(G.at[par], RO.at[2], YL)

    ly = []
    block = place(0, True)
    for k in range(C):
        at = pl.ds(k * RC, RC)
        directs[0, k][0].wait_recv()
        directs[0, k][1].wait_recv()
        LO[block, at] = (
            LO[block, at].astype(F32) + LD[0, 0, at].astype(F32) + LD[0, 1, at].astype(F32)
        ).astype(BF)
        ly.append(cp.put(LO.at[block, at], LY.at[at], YH))

    g2a.wait_recv()
    g2b.wait_recv()
    for side, dx, at in ((0, 1, pl.ds(0, CUT)), (1, -1, pl.ds(CUT, FF - CUT))):
        block = tok(dx, False)
        G[block, at] = (G[block, at].astype(F32) + RAB[at].astype(F32)).astype(BF)
        sent = cp.put(G.at[block], RO.at[side], X(dx))
        if side == 0:
            g5p = sent
        else:
            g5m = sent

    outs.append(weight_grad(1))

    block = j
    pair(block)
    sw = []
    for k in range(C):
        at = pl.ds(k * RC, RC)
        directs[1, k][0].wait_recv()
        directs[1, k][1].wait_recv()
        ly[k].wait_recv()
        FIN[at] = (
            LO[block, at].astype(F32) + LD[1, 0, at].astype(F32) + LD[1, 1, at].astype(F32) + LY[at].astype(F32)
        ).astype(BF)
        sw.append(cp.put_or_keep(sw_keep, FIN.at[at], SWP.at[at], SW, SWP.at[at]))
    outs[0].wait()
    outs.append(weight_grad(2))
    outs[1].wait()
    outs.append(weight_grad(3))

    for k in range(C):
        sw[k]()
        at = pl.ds(k * RC, RC)
        for r in range(0, TOK, 128):
            lay_stage[r : r + 128, k * RC : (k + 1) * RC] = SWP[at, r : r + 128].astype(F32).T.astype(BF)
    copy = pltpu.make_async_copy(lay_stage, lay_out, out_sem.at[4])
    copy.start()
    outs.append(copy)

    g4.wait_recv()
    g5p.wait_recv()
    g5m.wait_recv()

    def finish(k, _):
        rows = pl.ds(pl.multiple_of(k * 128, 128), 128)
        total = G[dp, :, rows].astype(F32)
        for side in range(3):
            total = total + RO[side, :, rows].astype(F32)
        total = total.T
        g = gate[rows, :].astype(F32)
        squash = jax.nn.sigmoid(g)
        gu_stage[rows, :] = (total * g * squash).astype(BF)
        gg_stage[rows, :] = (
            total * up[rows, :].astype(F32) * squash * (1.0 + g * (1.0 - squash))
        ).astype(BF)
        return 0

    lax.fori_loop(0, 4, finish, 0)
    for n, (stage, out) in enumerate(((gg_stage, gg_out), (gu_stage, gu_out))):
        copy = pltpu.make_async_copy(stage, out, out_sem.at[5 + n])
        copy.start()
        outs.append(copy)
    cp.finish()
    for copy in outs[2:]:
        copy.wait()


def shards(gate_pre, up_pre, w_down, cotangent):
    vmem = pl.BlockSpec(memory_space=pltpu.VMEM)
    anywhere = pl.BlockSpec(memory_space=pl.ANY)
    n_copies = 100
    flops = 2 * 3 * TOK * FF * 8192
    return pl.pallas_call(
        kernel,
        out_shape=(
            jax.ShapeDtypeStruct((TOK, HALF), BF),
            jax.ShapeDtypeStruct((TOK, FF), BF),
            jax.ShapeDtypeStruct((TOK, FF), BF),
            jax.ShapeDtypeStruct((FF, DM), BF),
        ),
        in_specs=[vmem] * 4,
        out_specs=[anywhere] * 4,
        scratch_shapes=[
            pltpu.VMEM((8, FF, TOK), BF),
            pltpu.VMEM((8, DM, TOK), BF),
            pltpu.VMEM((DM, FF), BF),
            pltpu.VMEM((HALF, TOK), BF),
            pltpu.VMEM((HALF, TOK), BF),
            pltpu.VMEM((8, FF, TOK), BF),
            pltpu.VMEM((FF, TOK), BF),
            pltpu.VMEM((2, FF, TOK), BF),
            pltpu.VMEM((FF, TOK), BF),
            pltpu.VMEM((3, FF, TOK), BF),
            pltpu.VMEM((8, HALF, TOK), BF),
            pltpu.VMEM((8, HALF, TOK), BF),
            pltpu.VMEM((8, HALF, TOK), BF),
            pltpu.VMEM((2, 2, C, HC, TOK), BF),
            pltpu.VMEM((2, 2, HALF, TOK), BF),
            pltpu.VMEM((HALF, TOK), BF),
            pltpu.VMEM((HALF, TOK), BF),
            pltpu.VMEM((HALF, TOK), BF),
            pltpu.VMEM((FF, 256), F32),
            pltpu.VMEM((2, FF, 256), BF),
            pltpu.VMEM((TOK, HALF), BF),
            pltpu.VMEM((TOK, FF), BF),
            pltpu.VMEM((TOK, FF), BF),
            pltpu.SemaphoreType.DMA((n_copies,)),
            pltpu.SemaphoreType.DMA((n_copies,)),
            pltpu.SemaphoreType.DMA((7,)),
        ],
        compiler_params=pltpu.CompilerParams(
            collective_id=0, has_side_effects=True, vmem_limit_bytes=64 * 2**20
        ),
        cost_estimate=pl.CostEstimate(flops=flops, bytes_accessed=2**24, transcendentals=0),
    )(gate_pre, up_pre, w_down, cotangent)


def solution(mesh):
    placed = (P("dp", "tensor"), P("dp", "tensor"), P("tensor", "dp"), P("dp", "tensor"))
    return jax.shard_map(
        shards,
        mesh=mesh,
        in_specs=placed,
        out_specs=(P("dp", "tensor"), P("dp", "tensor"), P("dp", "tensor"), P("tensor", "dp")),
        check_vma=False,
    )
```

time: 800 us -> 186 us (0.23)
  the two profiles are of different devices: /device:TPU:1 before, /device:TPU:77 now
where the time goes in v1:
time: 186 us
  Pallas kernels  176 us (95%)
  local copies, waits for them, and re-layouts  9.35 us (5%)
    pallas_call x1, Pallas kernels, shards(): pl.pallas_call(kernel, out_shape=(jax.ShapeDtypeStruct((TOK, HALF), BF),...  176 us
    unnamed x12, local copies, waits for them, and re-layouts  5.72 us

profile of v1, /device:TPU:77, one launch (start us, length us, event | category | flops | bytes accessed | tf_op | source)
XLA Modules:
  0.0 185.6 jit_solution(16058349332683302198)
XLA Ops:
  0.6 0.0 copy-start.2
  0.6 2.3 %copy.8.gate = bf16[512,928]{1,0:T(8,128)(2,1)} copy(bf16[512,928]{0,1:T(8,128)(2,1)} %param.4) | data formatting | bytes 1900544 | tf_op args[0]
  3.0 0.0 copy-done.2
  3.0 1.3 copy.9.up
  4.3 175.6 %shard_map.75 = (bf16[512,512]{1,0:T(8,128)(2,1)}, bf16[512,928]{1,0:T(8,128)(2,1)}, bf16[512,928]{1,0:T(8,128)(2,1)}, bf16[928,1024]{1,0:T(8,128)(2,1)}) custom-call(bf16[512,928]{1,0:T(8,128)(2,1)} %copy.8.gate, bf16[512,928]{1,0:T(8,128)(2,1)} %copy.9.up, bf16[928,1024]{1,0:T(8,128)(2,1)} %w.1, bf16[512,512]{1,0:T(8,128)(2,1)} %cot.1), custom_call_target="tpu_custom_call" | custom-call | flops 23353884672 | bytes 16777216 | tf_op jit(solution)/shard_map/pallas_call | solution.py:414
  179.9 0.0 copy-start.1
  179.9 0.0 copy-start.3
  179.9 2.4 %copy.10 = bf16[512,928]{0,1:T(8,128)(2,1)} copy(bf16[512,928]{1,0:T(8,128)(2,1)} %get-tuple-element.5) | data formatting | bytes 1900544 | tf_op jit(solution)/shard_map/pallas_call | solution.py:414
  182.2 0.0 copy-done.1
  182.2 0.0 copy-start
  182.3 1.3 copy.11
  183.5 0.0 copy-done.3
  183.5 0.8 copy.14
  184.3 0.0 copy-done
  184.3 1.2 copy.15
Async XLA Ops:
  0.6 2.4 %copy-start.2 = (bf16[512,928]{0,1:T(8,128)(2,1)S(1)}, bf16[512,928]{0,1:T(8,128)(2,1)}, u32[]{:S(2)}) copy-start(bf16[512,928]{0,1:T(8,128)(2,1)} %param.5) | copy-start | bytes 2850820
  179.9 2.4 %copy-start.1 = (bf16[512,928]{1,0:T(8,128)(2,1)S(1)}, bf16[512,928]{1,0:T(8,128)(2,1)}, u32[]{:S(2)}) copy-start(bf16[512,928]{1,0:T(8,128)(2,1)} %get-tuple-element.6) | copy-start | bytes 2850820
  179.9 3.7 %copy-start.3 = (bf16[512,512]{1,0:T(8,128)(2,1)S(1)}, bf16[512,512]{1,0:T(8,128)(2,1)}, u32[]{:S(2)}) copy-start(bf16[512,512]{1,0:T(8,128)(2,1)} %get-tuple-element.12) | copy-start | bytes 1572868
  182.2 2.1 %copy-start = (bf16[928,1024]{1,0:T(8,128)(2,1)S(1)}, bf16[928,1024]{1,0:T(8,128)(2,1)}, u32[]{:S(2)}) copy-start(bf16[928,1024]{1,0:T(8,128)(2,1)} %get-tuple-element.15) | copy-start | bytes 5701636

commit v2 on v1

--- a/solution.py
+++ b/solution.py
@@ -74,9 +74,9 @@
 
 
 def kernel(
-    gate, up, w, cot, lay_out, gg_out, gu_out, gd_out,
-    HT, CT, WT, OWN, ZM, G, R1, R3, RAB, RO, LO, LS, LX, LH, LD, LY, FIN, SWP,
-    acc, gd_stage, lay_stage, gg_stage, gu_stage, send_sem, recv_sem, out_sem,
+    gate_in, up_in, w_in, cot_in, lay_out, gg_out, gu_out, gd_out,
+    gate, up, w, cot, HT, CT, WT, OWN, ZM, G, R1, R3, RAB, RO, LO, LS, LX, LH, LD, LY, FIN, SWP,
+    acc, gd_stage, lay_stage, gg_stage, gu_stage, send_sem, recv_sem, in_sem, out_sem,
 ):
     dp, t = lax.axis_index("dp"), lax.axis_index("tensor")
     x, yl = dp // 2, dp % 2
@@ -122,39 +122,46 @@
     greeted = (X(1), X(-1), YL, Z(1), Z(-1), YH, CORE, T1, T1S, T2, T2S, SW, SWS)
     for other in greeted:
         pl.semaphore_signal(barrier, inc=1, device_id=other, device_id_type=MESH)
-
+    loads = []
+    for n, (src, dst) in enumerate(((cot_in, cot), (gate_in, gate), (up_in, up), (w_in, w))):
+        loads.append(pltpu.make_async_copy(src, dst, in_sem.at[n]))
+        loads[-1].start()
+
+    loads[0].wait()
     for r in range(0, HALF, 128):
         OWN[:, r : r + 128] = cot[r : r + 128, :].astype(F32).T.astype(BF)
+    loads[1].wait()
+    loads[2].wait()
 
     def make_hidden(k, _):
-        rows = pl.ds(pl.multiple_of(k * 128, 128), 128)
+        rows = pl.ds(pl.multiple_of(k * 32, 32), 32)
         g = gate[rows, :].astype(F32)
-        h = g * jax.nn.sigmoid(g) * up[rows, :].astype(F32)
-        HT[dp, :, rows] = h.T.astype(BF)
+        HT[dp, rows, :] = (g * jax.nn.sigmoid(g) * up[rows, :].astype(F32)).astype(BF)
         return 0
-
-    lax.fori_loop(0, 4, make_hidden, 0)
 
     pl.semaphore_wait(barrier, len(greeted))
     cp = Copies(send_sem, recv_sem)
-
-    def piece(ref, *at, k):
-        return ref.at[(*at, pl.ds(k * RC, RC))]
+    low, high = pl.ds(0, CUT), pl.ds(CUT, FF - CUT)
 
     def crow(k, size=RC):
         return pl.ds(pl.multiple_of(c * HALF + k, 16), size)
 
-    t1 = [cp.put_or_keep(t1_keep, OWN.at[pl.ds(k * RC, RC)], ZM.at[pl.ds(k * RC, RC)], T1, ZM.at[pl.ds(k * RC, RC)]) for k in range(C)]
-    own = HT.at[dp]
-    s1y = cp.put(own, own, YL, HT.at[tok(0, True)])
-    s1p = cp.put(own, own, X(1), HT.at[tok(-1, False)])
-    s1m = cp.put(own, own, X(-1), HT.at[tok(1, False)])
-
-    for r in range(0, FF, 464):
-        WT[:, r : r + 464] = w[r : r + 464, :].astype(F32).T.astype(BF)
-
-    t2_place = (T2[1] // 2)
-    t2 = []
+    def share(ref, target):
+        return cp.put(ref, ref, target)
+
+    t1, t2 = [], []
+    for k in range(C):
+        at = pl.ds(k * RC, RC)
+        t1.append(cp.put_or_keep(t1_keep, OWN.at[at], ZM.at[at], T1, ZM.at[at]))
+    lax.fori_loop(0, 29, make_hidden, 0)
+    s1p, s1m = [share(HT.at[dp, low], X(1))], [share(HT.at[dp, high], X(-1))]
+    s1y = share(HT.at[dp], YL)
+
+    loads[3].wait()
+    for r in range(0, FF, CUT):
+        WT[:, r : r + CUT] = w[r : r + CUT, :].astype(F32).T.astype(BF)
+
+    t2_place = T2[1] // 2
     for k in range(C):
         t1[k]()
         t2.append(cp.put_or_keep(t2_keep, ZM.at[pl.ds(k * RC, RC)], CT.at[t2_place, crow(k * RC)], T2, CT.at[j, crow(k * RC)]))
@@ -176,74 +183,62 @@
 
     lx = [make_layer(dp)]
 
+    s1p[0].wait_recv()
+    s1m[0].wait_recv()
+    s2 = [share(HT.at[tok(-1, False), low], X(1)), share(HT.at[tok(1, False), high], X(-1))]
+    s1p.append(share(HT.at[dp, high], X(1)))
+    s1m.append(share(HT.at[dp, low], X(-1)))
+
     def spread(block, k):
         ref = CT.at[block, crow(k * RC)]
-        return cp.put(ref, ref, Z(1)), cp.put(ref, ref, Z(-1))
+        return share(ref, Z(1)), share(ref, Z(-1))
 
     def forward(row, k):
         a = CT.at[place(-1, row), crow(k * RC, HC)]
         b = CT.at[place(1, row), crow(k * RC + HC, HC)]
-        return cp.put(a, a, Z(1)), cp.put(b, b, Z(-1))
-
-    t3, near_own, near_par = [], [], []
+        return share(a, Z(1)), share(b, Z(-1))
+
+    t3, t5, near = [], [], {}
+
+    def cross(block):
+        t5.append(share(CT.at[block, crow(0, HALF)], CORE))
+
     for k in range(C):
         t2[k]()
-        ref = CT.at[j, crow(k * RC)]
-        t3.append(cp.put(ref, ref, YH))
-        near_own.append(spread(j, k))
-    t5 = []
-
-    def cross(block):
-        ref = CT.at[block, crow(0, HALF)]
-        t5.append(cp.put(ref, ref, CORE))
-
+        t3.append(share(CT.at[j, crow(k * RC)], YH))
+        near[False, k] = spread(j, k)
     cross(j)
-
-    s1p.wait_recv()
-    a = HT.at[tok(-1, False), pl.ds(0, CUT)]
-    s2a = cp.put(a, a, X(1))
-    s1m.wait_recv()
-    b = HT.at[tok(1, False), pl.ds(CUT, FF - CUT)]
-    s2b = cp.put(b, b, X(-1))
     s1y.wait_recv()
     par = HT.at[tok(0, True)]
-    s3p = cp.put(par, par, X(1))
-    s3m = cp.put(par, par, X(-1))
+    s3p, s3m = share(par, X(1)), share(par, X(-1))
 
     for k in range(C):
         t3[k].wait_recv()
-        near_par.append(spread(place(0, True), k))
+        near[True, k] = spread(place(0, True), k)
+    s2[0].wait_recv()
+    s2[1].wait_recv()
+    s4 = share(HT.at[tok(2, False)], YL)
     cross(place(0, True))
-
     lx.append(make_layer(tok(0, True)))
+    lx.append(make_layer(tok(2, False)))
+
+    far = {}
+    for row in (False, True):
+        for k in range(C):
+            near[row, k][0].wait_recv()
+            near[row, k][1].wait_recv()
+            far[row, k] = forward(row, k)
+        cross(place(1, row))
+        cross(place(-1, row))
+    s1p[1].wait_recv()
+    s1m[1].wait_recv()
     lx.append(make_layer(tok(1, False)))
     lx.append(make_layer(tok(-1, False)))
-
-    far = []
-    for row, near in ((False, near_own), (True, near_par)):
+    for row in (False, True):
         for k in range(C):
-            near[k][0].wait_recv()
-            near[k][1].wait_recv()
-            far.extend(forward(row, k))
-        cross(place(1, row))
-        cross(place(-1, row))
-
-    s2a.wait_recv()
-    s2b.wait_recv()
-    two = HT.at[tok(2, False)]
-    s4 = cp.put(two, two, YL)
-    lx.append(make_layer(tok(2, False)))
-
-    for f in far[: 2 * C]:
-        f.wait_recv()
-    cross(place(2, False))
-    for f in far[2 * C :]:
-        f.wait_recv()
-    cross(place(2, True))
-    s3p.wait_recv()
-    s3m.wait_recv()
-    lx.append(make_layer(tok(1, True)))
-    lx.append(make_layer(tok(-1, True)))
+            far[row, k][0].wait_recv()
+            far[row, k][1].wait_recv()
+        cross(place(2, row))
     for f in t5:
         f.wait_recv()
 
@@ -257,15 +252,21 @@
 
         lax.fori_loop(0, 2, part, 0)
 
+    make_grad(tok(2, True))
+    g1 = cp.put(G.at[tok(2, True)], R1, YL)
     make_grad(tok(1, True))
     g3p = cp.put(G.at[tok(1, True)], R3.at[0], X(1))
     make_grad(tok(-1, True))
     g3m = cp.put(G.at[tok(-1, True)], R3.at[1], X(-1))
-    make_grad(tok(2, True))
-    g1 = cp.put(G.at[tok(2, True)], R1, YL)
+    for g in (tok(2, False), tok(1, False), tok(-1, False), tok(0, True), dp):
+        make_grad(g)
+
     s4.wait_recv()
     lx.append(make_layer(tok(2, True)))
-
+    s3p.wait_recv()
+    lx.append(make_layer(tok(-1, True)))
+    s3m.wait_recv()
+    lx.append(make_layer(tok(1, True)))
     for f in lx:
         f.wait_recv()
 
@@ -281,30 +282,26 @@
                 cp.put(LO.at[two, pl.ds(k * RC, HC)], LH.at[n, 0, k], Z(1)),
                 cp.put(LO.at[two, pl.ds(k * RC + HC, HC)], LH.at[n, 1, k], Z(-1)),
             )
+    for row in (True, False):
         pair(place(1, row))
         pair(place(-1, row))
-    for dx in (2, 1, -1):
-        make_grad(tok(dx, False))
+
+    def relay(n, row, k):
+        sent = []
+        for side, dz in ((0, 1), (1, -1)):
+            block = place(dz, row)
+            halves[n, k][side].wait_recv()
+            at = pl.ds(k * RC + side * HC, HC)
+            LO[block, at] = (LO[block, at].astype(F32) + LH[n, side, k].astype(F32)).astype(BF)
+            at = pl.ds(k * RC, RC)
+            sent.append(cp.put(LO.at[block, at], LD.at[n, side, at], Z(dz)))
+        directs[n, k] = sent
+
     for n, row in enumerate((True, False)):
         for k in range(C):
-            sent = []
-            for side, dz in ((0, 1), (1, -1)):
-                block = place(dz, row)
-                halves[n, k][side].wait_recv()
-                at = pl.ds(k * RC + side * HC, HC)
-                LO[block, at] = (LO[block, at].astype(F32) + LH[n, side, k].astype(F32)).astype(BF)
-                at = pl.ds(k * RC, RC)
-                sent.append(cp.put(LO.at[block, at], LD.at[n, side, at], Z(dz)))
-            directs[n, k] = sent
+            relay(n, row, k)
     pair(place(0, True))
-    make_grad(tok(0, True))
-
-    g1.wait_recv()
-    two = tok(2, False)
-    G[two] = (G[two].astype(F32) + R1[...].astype(F32)).astype(BF)
-    g2a = cp.put(G.at[two, pl.ds(0, CUT)], RAB.at[pl.ds(0, CUT)], X(1))
-    g2b = cp.put(G.at[two, pl.ds(CUT, FF - CUT)], RAB.at[pl.ds(CUT, FF - CUT)], X(-1))
-    make_grad(dp)
+    pair(j)
 
     def weight_grad(n):
         cols = pl.ds(n * 256, 256)
@@ -321,12 +318,13 @@
         return copy
 
     outs = [weight_grad(0)]
-
-    g3p.wait_recv()
-    g3m.wait_recv()
-    par = tok(0, True)
-    G[par] = (G[par].astype(F32) + R3[0].astype(F32) + R3[1].astype(F32)).astype(BF)
-    g4 = cp.put(G.at[par], RO.at[2], YL)
+    g1.wait_recv()
+    two = tok(2, False)
+    G[two] = (G[two].astype(F32) + R1[...].astype(F32)).astype(BF)
+    g2a = cp.put(G.at[two, low], RAB.at[low], X(1))
+    g2b = cp.put(G.at[two, high], RAB.at[high], X(-1))
+    up_one, down_one = tok(1, False), tok(-1, False)
+    g5 = [cp.put(G.at[up_one, high], RO.at[0, high], X(1)), cp.put(G.at[down_one, low], RO.at[1, low], X(-1))]
 
     ly = []
     block = place(0, True)
@@ -338,22 +336,14 @@
             LO[block, at].astype(F32) + LD[0, 0, at].astype(F32) + LD[0, 1, at].astype(F32)
         ).astype(BF)
         ly.append(cp.put(LO.at[block, at], LY.at[at], YH))
-
-    g2a.wait_recv()
-    g2b.wait_recv()
-    for side, dx, at in ((0, 1, pl.ds(0, CUT)), (1, -1, pl.ds(CUT, FF - CUT))):
-        block = tok(dx, False)
-        G[block, at] = (G[block, at].astype(F32) + RAB[at].astype(F32)).astype(BF)
-        sent = cp.put(G.at[block], RO.at[side], X(dx))
-        if side == 0:
-            g5p = sent
-        else:
-            g5m = sent
+    g3p.wait_recv()
+    g3m.wait_recv()
+    par = tok(0, True)
+    G[par] = (G[par].astype(F32) + R3[0].astype(F32) + R3[1].astype(F32)).astype(BF)
+    g5.append(cp.put(G.at[par], RO.at[2], YL))
 
     outs.append(weight_grad(1))
 
-    block = j
-    pair(block)
     sw = []
     for k in range(C):
         at = pl.ds(k * RC, RC)
@@ -361,9 +351,17 @@
         directs[1, k][1].wait_recv()
         ly[k].wait_recv()
         FIN[at] = (
-            LO[block, at].astype(F32) + LD[1, 0, at].astype(F32) + LD[1, 1, at].astype(F32) + LY[at].astype(F32)
+            LO[j, at].astype(F32) + LD[1, 0, at].astype(F32) + LD[1, 1, at].astype(F32) + LY[at].astype(F32)
         ).astype(BF)
         sw.append(cp.put_or_keep(sw_keep, FIN.at[at], SWP.at[at], SW, SWP.at[at]))
+
+    g2a.wait_recv()
+    G[up_one, low] = (G[up_one, low].astype(F32) + RAB[low].astype(F32)).astype(BF)
+    g5.append(cp.put(G.at[up_one, low], RO.at[0, low], X(1)))
+    g2b.wait_recv()
+    G[down_one, high] = (G[down_one, high].astype(F32) + RAB[high].astype(F32)).astype(BF)
+    g5.append(cp.put(G.at[down_one, high], RO.at[1, high], X(-1)))
+
     outs[0].wait()
     outs.append(weight_grad(2))
     outs[1].wait()
@@ -378,16 +376,14 @@
     copy.start()
     outs.append(copy)
 
-    g4.wait_recv()
-    g5p.wait_recv()
-    g5m.wait_recv()
+    for f in g5:
+        f.wait_recv()
 
     def finish(k, _):
-        rows = pl.ds(pl.multiple_of(k * 128, 128), 128)
-        total = G[dp, :, rows].astype(F32)
+        rows = pl.ds(pl.multiple_of(k * 32, 32), 32)
+        total = G[dp, rows, :].astype(F32)
         for side in range(3):
-            total = total + RO[side, :, rows].astype(F32)
-        total = total.T
+            total = total + RO[side, rows, :].astype(F32)
         g = gate[rows, :].astype(F32)
         squash = jax.nn.sigmoid(g)
         gu_stage[rows, :] = (total * g * squash).astype(BF)
@@ -396,7 +392,7 @@
         ).astype(BF)
         return 0
 
-    lax.fori_loop(0, 4, finish, 0)
+    lax.fori_loop(0, 29, finish, 0)
     for n, (stage, out) in enumerate(((gg_stage, gg_out), (gu_stage, gu_out))):
         copy = pltpu.make_async_copy(stage, out, out_sem.at[5 + n])
         copy.start()
@@ -407,21 +403,24 @@
 
 
 def shards(gate_pre, up_pre, w_down, cotangent):
-    vmem = pl.BlockSpec(memory_space=pltpu.VMEM)
     anywhere = pl.BlockSpec(memory_space=pl.ANY)
     n_copies = 100
     flops = 2 * 3 * TOK * FF * 8192
-    return pl.pallas_call(
+    layer_out, grad_gate, grad_up, grad_down = pl.pallas_call(
         kernel,
         out_shape=(
             jax.ShapeDtypeStruct((TOK, HALF), BF),
-            jax.ShapeDtypeStruct((TOK, FF), BF),
-            jax.ShapeDtypeStruct((TOK, FF), BF),
+            jax.ShapeDtypeStruct((FF, TOK), BF),
+            jax.ShapeDtypeStruct((FF, TOK), BF),
             jax.ShapeDtypeStruct((FF, DM), BF),
         ),
-        in_specs=[vmem] * 4,
+        in_specs=[anywhere] * 4,
         out_specs=[anywhere] * 4,
         scratch_shapes=[
+            pltpu.VMEM((FF, TOK), BF),
+            pltpu.VMEM((FF, TOK), BF),
+            pltpu.VMEM((FF, DM), BF),
+            pltpu.VMEM((TOK, HALF), BF),
             pltpu.VMEM((8, FF, TOK), BF),
             pltpu.VMEM((8, DM, TOK), BF),
             pltpu.VMEM((DM, FF), BF),
@@ -443,17 +442,19 @@
             pltpu.VMEM((FF, 256), F32),
             pltpu.VMEM((2, FF, 256), BF),
             pltpu.VMEM((TOK, HALF), BF),
-            pltpu.VMEM((TOK, FF), BF),
-            pltpu.VMEM((TOK, FF), BF),
+            pltpu.VMEM((FF, TOK), BF),
+            pltpu.VMEM((FF, TOK), BF),
             pltpu.SemaphoreType.DMA((n_copies,)),
             pltpu.SemaphoreType.DMA((n_copies,)),
+            pltpu.SemaphoreType.DMA((4,)),
             pltpu.SemaphoreType.DMA((7,)),
         ],
         compiler_params=pltpu.CompilerParams(
             collective_id=0, has_side_effects=True, vmem_limit_bytes=64 * 2**20
         ),
         cost_estimate=pl.CostEstimate(flops=flops, bytes_accessed=2**24, transcendentals=0),
-    )(gate_pre, up_pre, w_down, cotangent)
+    )(gate_pre.T, up_pre.T, w_down, cotangent)
+    return layer_out, grad_gate.T, grad_up.T, grad_down
 
 
 def solution(mesh):

time: 186 us -> 165 us (0.89)
  the two profiles are of different devices: /device:TPU:77 before, /device:TPU:34 now
where the time goes in v2:
time: 165 us
  Pallas kernels  158 us (96%)
  local copies, waits for them, and re-layouts  6.46 us (4%)
    pallas_call x1, Pallas kernels, shards(): pl.pallas_call(kernel, out_shape=(jax.ShapeDtypeStruct((TOK, HALF), BF),...  158 us
    unnamed x8, local copies, waits for them, and re-layouts  6.46 us

profile of v2, /device:TPU:34, one launch (start us, length us, event | category | flops | bytes accessed | tf_op | source)
XLA Modules:
  0.0 164.7 jit_solution(6415170380845844139)
XLA Ops:
  0.6 157.6 %shard_map.75 = (bf16[512,512]{1,0:T(8,128)(2,1)}, bf16[928,512]{1,0:T(8,128)(2,1)}, bf16[928,512]{1,0:T(8,128)(2,1)}, bf16[928,1024]{1,0:T(8,128)(2,1)}) custom-call(bf16[928,512]{1,0:T(8,128)(2,1)} %bitcast.6, bf16[928,512]{1,0:T(8,128)(2,1)} %bitcast.7, bf16[928,1024]{1,0:T(8,128)(2,1)} %w_in.1, bf16[512,512]{1,0:T(8,128)(2,1)} %cot_in.1), custom_call_target="tpu_custom_call" | custom-call | flops 23353884672 | bytes 16777216 | tf_op jit(solution)/shard_map/pallas_call | solution.py:409
  158.2 0.0 copy-start.1
  158.2 2.0 %copy.12 = bf16[512,512]{1,0:T(8,128)(2,1)} copy(bf16[512,512]{1,0:T(8,128)(2,1)} %get-tuple-element.16) | data formatting | bytes 1048576
  160.2 0.0 copy-start
  160.2 2.3 %copy.13 = bf16[512,928]{0,1:T(8,128)(2,1)} copy(bf16[512,928]{0,1:T(8,128)(2,1)} %bitcast.5) | data formatting | bytes 1900544
  162.5 0.0 copy-done.1
  162.5 0.9 copy.14
  163.4 0.0 copy-done
  163.4 1.2 copy.15
Async XLA Ops:
  158.2 4.3 %copy-start.1 = (bf16[928,512]{1,0:T(8,128)(2,1)S(1)}, bf16[928,512]{1,0:T(8,128)(2,1)}, u32[]{:S(2)}) copy-start(bf16[928,512]{1,0:T(8,128)(2,1)} %get-tuple-element.10) | copy-start | bytes 2850820
  160.2 3.3 %copy-start = (bf16[928,1024]{1,0:T(8,128)(2,1)S(1)}, bf16[928,1024]{1,0:T(8,128)(2,1)}, u32[]{:S(2)}) copy-start(bf16[928,1024]{1,0:T(8,128)(2,1)} %get-tuple-element.19) | copy-start | bytes 5701636

commit v3 on v2

--- a/solution.py
+++ b/solution.py
@@ -92,34 +92,31 @@
     YL = (x * 2 + 1 - yl, t)
     YH = (dp, (1 - yh) * 8 + z * 2 + c)
     CORE = (dp, t + 1 - 2 * c)
-    T1, T1S = Z(x), Z(4 - x)
-    zs = (z - x + 4) % 4
-    T2 = ((2 * yh + zs // 2) * 2 + zs % 2, ((yl + yh + zs) % 2) * 8 + z * 2 + c)
-    zo = 2 * (x % 2) + yl
-    xs, yls = (z - zo + 4) % 4, (yh + x // 2 + yl) % 2
-    T2S = (xs * 2 + yls, (x // 2) * 8 + z * 2 + c)
-    q = xs * 2 + yls
-    SW = (q, 2 * dp + c)
-    xi, yli = j // 2, j % 2
-    zi = 2 * (xi % 2) + yli
-    SWS = (j, ((yl + xi // 2 + yli) % 2) * 8 + ((x + zi) % 4) * 2 + c)
-    t1_keep = x == 0
-    t2_keep = jnp.logical_and(T2[0] == dp, T2[1] == t)
-    sw_keep = jnp.logical_and(SW[0] == dp, SW[1] == t)
+    x1, x0, z1, z0 = x // 2, x % 2, z // 2, z % 2
+    T1, T1S, T2, SW, SWS, q = [], [], [], [], [], []
+    for k in range(C):
+        there = ((yl + yh + z0) % 2) * 8 + (2 * ((x1 + yh + k) % 2) + (x0 + z1) % 2) * 2 + c
+        T1.append((x * 2 + z0, there))
+        hi, lo = (z1 + x1 + k) % 2, (z0 + x0) % 2
+        T1S.append((x * 2 + (yh + hi + yl) % 2, hi * 8 + (2 * lo + yl) * 2 + c))
+        T2.append(((2 * hi + lo) * 2 + yl, t))
+        q.append((2 * hi + lo) * 2 + (yh + x1 + yl) % 2)
+        SW.append((q[k], 2 * dp + c))
+        SWS.append((j, there))
+
+    def here(device):
+        return jnp.logical_and(device[0] == dp, device[1] == t)
 
     def tok(dx, other):
         row = 1 - yl if other else yl
         return ((x + dx + 4) % 4) * 2 + row
 
-    def slot(g):
-        return ((g % 2 + x // 2 + yl) % 2) * 4 + (g // 2 + zo) % 4
-
-    def place(dz, other):
-        row = 1 - yh if other else yh
-        return row * 4 + (z + dz + 4) % 4
+    def place(dz, other, k):
+        row, at = (1 - yh if other else yh), (z + dz + 4) % 4
+        return (2 * ((at // 2 + x1 + k) % 2) + (at + x0) % 2) * 2 + (row + x1 + yl) % 2
 
     barrier = pltpu.get_barrier_semaphore()
-    greeted = (X(1), X(-1), YL, Z(1), Z(-1), YH, CORE, T1, T1S, T2, T2S, SW, SWS)
+    greeted = (X(1), X(-1), YL, Z(1), Z(-1), YH, CORE, *T1, *T1S, *T2, *SW, *SWS)
     for other in greeted:
         pl.semaphore_signal(barrier, inc=1, device_id=other, device_id_type=MESH)
     loads = []
@@ -152,7 +149,7 @@
     t1, t2 = [], []
     for k in range(C):
         at = pl.ds(k * RC, RC)
-        t1.append(cp.put_or_keep(t1_keep, OWN.at[at], ZM.at[at], T1, ZM.at[at]))
+        t1.append(cp.put_or_keep(here(T1[k]), OWN.at[at], ZM.at[at], T1[k], ZM.at[at]))
     lax.fori_loop(0, 29, make_hidden, 0)
     s1p, s1m = [share(HT.at[dp, low], X(1))], [share(HT.at[dp, high], X(-1))]
     s1y = share(HT.at[dp], YL)
@@ -161,25 +158,22 @@
     for r in range(0, FF, CUT):
         WT[:, r : r + CUT] = w[r : r + CUT, :].astype(F32).T.astype(BF)
 
-    t2_place = T2[1] // 2
     for k in range(C):
         t1[k]()
-        t2.append(cp.put_or_keep(t2_keep, ZM.at[pl.ds(k * RC, RC)], CT.at[t2_place, crow(k * RC)], T2, CT.at[j, crow(k * RC)]))
+        t2.append(cp.put_or_keep(here(T2[k]), ZM.at[pl.ds(k * RC, RC)], CT.at[T1S[k][0], crow(k * RC)], T2[k], CT.at[q[k], crow(k * RC)]))
 
     def make_layer(g):
-        s = slot(g)
-
         def part(k, _):
             cols = pl.ds(pl.multiple_of(k * 256, 256), 256)
             here = pl.ds(pl.multiple_of(c * HALF, HALF), HALF)
             there = pl.ds(pl.multiple_of((1 - c) * HALF, HALF), HALF)
             h = HT[g, :, cols]
-            LS[s, :, cols] = nn(WT[there, :], h).astype(BF)
-            LO[s, :, cols] = nn(WT[here, :], h).astype(BF)
+            LS[g, :, cols] = nn(WT[there, :], h).astype(BF)
+            LO[g, :, cols] = nn(WT[here, :], h).astype(BF)
             return 0
 
         lax.fori_loop(0, 2, part, 0)
-        return cp.put(LS.at[s], LX.at[s], CORE)
+        return cp.put(LS.at[g], LX.at[g], CORE)
 
     lx = [make_layer(dp)]
 
@@ -189,36 +183,36 @@
     s1p.append(share(HT.at[dp, high], X(1)))
     s1m.append(share(HT.at[dp, low], X(-1)))
 
-    def spread(block, k):
-        ref = CT.at[block, crow(k * RC)]
+    def spread(row, k):
+        ref = CT.at[place(0, row, k), crow(k * RC)]
         return share(ref, Z(1)), share(ref, Z(-1))
 
     def forward(row, k):
-        a = CT.at[place(-1, row), crow(k * RC, HC)]
-        b = CT.at[place(1, row), crow(k * RC + HC, HC)]
+        a = CT.at[place(-1, row, k), crow(k * RC, HC)]
+        b = CT.at[place(1, row, k), crow(k * RC + HC, HC)]
         return share(a, Z(1)), share(b, Z(-1))
 
     t3, t5, near = [], [], {}
 
-    def cross(block):
-        t5.append(share(CT.at[block, crow(0, HALF)], CORE))
+    def cross(dz, row, k):
+        t5.append(share(CT.at[place(dz, row, k), crow(k * RC)], CORE))
 
     for k in range(C):
         t2[k]()
-        t3.append(share(CT.at[j, crow(k * RC)], YH))
-        near[False, k] = spread(j, k)
-    cross(j)
+        t3.append(share(CT.at[q[k], crow(k * RC)], YH))
+        near[False, k] = spread(False, k)
+        cross(0, False, k)
     s1y.wait_recv()
     par = HT.at[tok(0, True)]
     s3p, s3m = share(par, X(1)), share(par, X(-1))
 
     for k in range(C):
         t3[k].wait_recv()
-        near[True, k] = spread(place(0, True), k)
+        near[True, k] = spread(True, k)
+        cross(0, True, k)
     s2[0].wait_recv()
     s2[1].wait_recv()
     s4 = share(HT.at[tok(2, False)], YL)
-    cross(place(0, True))
     lx.append(make_layer(tok(0, True)))
     lx.append(make_layer(tok(2, False)))
 
@@ -228,8 +222,8 @@
             near[row, k][0].wait_recv()
             near[row, k][1].wait_recv()
             far[row, k] = forward(row, k)
-        cross(place(1, row))
-        cross(place(-1, row))
+            cross(1, row, k)
+            cross(-1, row, k)
     s1p[1].wait_recv()
     s1m[1].wait_recv()
     lx.append(make_layer(tok(1, False)))
@@ -238,16 +232,14 @@
         for k in range(C):
             far[row, k][0].wait_recv()
             far[row, k][1].wait_recv()
-        cross(place(2, row))
+            cross(2, row, k)
     for f in t5:
         f.wait_recv()
 
     def make_grad(g):
-        s = slot(g)
-
         def part(k, _):
             cols = pl.ds(pl.multiple_of(k * 256, 256), 256)
-            G[g, :, cols] = nn(w[...], CT[s, :, cols]).astype(BF)
+            G[g, :, cols] = nn(w[...], CT[g, :, cols]).astype(BF)
             return 0
 
         lax.fori_loop(0, 2, part, 0)
@@ -258,9 +250,6 @@
     g3p = cp.put(G.at[tok(1, True)], R3.at[0], X(1))
     make_grad(tok(-1, True))
     g3m = cp.put(G.at[tok(-1, True)], R3.at[1], X(-1))
-    for g in (tok(2, False), tok(1, False), tok(-1, False), tok(0, True), dp):
-        make_grad(g)
-
     s4.wait_recv()
     lx.append(make_layer(tok(2, True)))
     s3p.wait_recv()
@@ -270,26 +259,29 @@
     for f in lx:
         f.wait_recv()
 
-    def pair(block):
-        LO[block] = (LO[block].astype(F32) + LX[block].astype(F32)).astype(BF)
+    def pair(dz, row, k):
+        block, at = place(dz, row, k), pl.ds(k * RC, RC)
+        LO[block, at] = (LO[block, at].astype(F32) + LX[block, at].astype(F32)).astype(BF)
 
     halves, directs = {}, {}
-    for n, row in enumerate((True, False)):
-        two = place(2, row)
-        pair(two)
+    rows = ((0, True), (1, False))
+    for n, row in rows:
         for k in range(C):
+            pair(2, row, k)
+            two = place(2, row, k)
             halves[n, k] = (
                 cp.put(LO.at[two, pl.ds(k * RC, HC)], LH.at[n, 0, k], Z(1)),
                 cp.put(LO.at[two, pl.ds(k * RC + HC, HC)], LH.at[n, 1, k], Z(-1)),
             )
-    for row in (True, False):
-        pair(place(1, row))
-        pair(place(-1, row))
+    for n, row in rows:
+        for k in range(C):
+            pair(1, row, k)
+            pair(-1, row, k)
 
     def relay(n, row, k):
         sent = []
         for side, dz in ((0, 1), (1, -1)):
-            block = place(dz, row)
+            block = place(dz, row, k)
             halves[n, k][side].wait_recv()
             at = pl.ds(k * RC + side * HC, HC)
             LO[block, at] = (LO[block, at].astype(F32) + LH[n, side, k].astype(F32)).astype(BF)
@@ -297,18 +289,20 @@
             sent.append(cp.put(LO.at[block, at], LD.at[n, side, at], Z(dz)))
         directs[n, k] = sent
 
-    for n, row in enumerate((True, False)):
+    make_grad(tok(2, False))
+    for n, row in rows:
         for k in range(C):
             relay(n, row, k)
-    pair(place(0, True))
-    pair(j)
+        if row:
+            make_grad(tok(1, False))
+            make_grad(tok(-1, False))
 
     def weight_grad(n):
         cols = pl.ds(n * 256, 256)
         acc[...] = jnp.zeros_like(acc)
 
         def add(g, _):
-            acc[...] += nt(HT[g], CT[slot(g), cols, :])
+            acc[...] += nt(HT[g], CT[g, cols, :])
             return 0
 
         lax.fori_loop(0, 8, add, 0)
@@ -317,7 +311,6 @@
         copy.start()
         return copy
 
-    outs = [weight_grad(0)]
     g1.wait_recv()
     two = tok(2, False)
     G[two] = (G[two].astype(F32) + R1[...].astype(F32)).astype(BF)
@@ -325,10 +318,14 @@
     g2b = cp.put(G.at[two, high], RAB.at[high], X(-1))
     up_one, down_one = tok(1, False), tok(-1, False)
     g5 = [cp.put(G.at[up_one, high], RO.at[0, high], X(1)), cp.put(G.at[down_one, low], RO.at[1, low], X(-1))]
-
-    ly = []
-    block = place(0, True)
-    for k in range(C):
+    for k in range(C):
+        pair(0, True, k)
+        pair(0, False, k)
+    make_grad(tok(0, True))
+
+    ly, outs = [], []
+    for k in range(C):
+        block = place(0, True, k)
         at = pl.ds(k * RC, RC)
         directs[0, k][0].wait_recv()
         directs[0, k][1].wait_recv()
@@ -336,12 +333,15 @@
             LO[block, at].astype(F32) + LD[0, 0, at].astype(F32) + LD[0, 1, at].astype(F32)
         ).astype(BF)
         ly.append(cp.put(LO.at[block, at], LY.at[at], YH))
+        if k == 0:
+            make_grad(dp)
     g3p.wait_recv()
     g3m.wait_recv()
     par = tok(0, True)
     G[par] = (G[par].astype(F32) + R3[0].astype(F32) + R3[1].astype(F32)).astype(BF)
     g5.append(cp.put(G.at[par], RO.at[2], YL))
 
+    outs.append(weight_grad(0))
     outs.append(weight_grad(1))
 
     sw = []
@@ -351,9 +351,9 @@
         directs[1, k][1].wait_recv()
         ly[k].wait_recv()
         FIN[at] = (
-            LO[j, at].astype(F32) + LD[1, 0, at].astype(F32) + LD[1, 1, at].astype(F32) + LY[at].astype(F32)
+            LO[q[k], at].astype(F32) + LD[1, 0, at].astype(F32) + LD[1, 1, at].astype(F32) + LY[at].astype(F32)
         ).astype(BF)
-        sw.append(cp.put_or_keep(sw_keep, FIN.at[at], SWP.at[at], SW, SWP.at[at]))
+        sw.append(cp.put_or_keep(here(SW[k]), FIN.at[at], SWP.at[at], SW[k], SWP.at[at]))
 
     g2a.wait_recv()
     G[up_one, low] = (G[up_one, low].astype(F32) + RAB[low].astype(F32)).astype(BF)
@@ -402,18 +402,32 @@
         copy.wait()
 
 
+def place_outputs(*refs):
+    sources, results, stages, sems = refs[:4], refs[4:8], refs[8:12], refs[12]
+    arrive = [pltpu.make_async_copy(sources[n], stages[n], sems.at[n]) for n in range(4)]
+    leave = [pltpu.make_async_copy(stages[n], results[n], sems.at[4 + n]) for n in range(4)]
+    for copy in arrive:
+        copy.start()
+    for n in range(4):
+        arrive[n].wait()
+        leave[n].start()
+    for copy in leave:
+        copy.wait()
+
+
 def shards(gate_pre, up_pre, w_down, cotangent):
     anywhere = pl.BlockSpec(memory_space=pl.ANY)
     n_copies = 100
     flops = 2 * 3 * TOK * FF * 8192
-    layer_out, grad_gate, grad_up, grad_down = pl.pallas_call(
+    shapes = (
+        jax.ShapeDtypeStruct((TOK, HALF), BF),
+        jax.ShapeDtypeStruct((FF, TOK), BF),
+        jax.ShapeDtypeStruct((FF, TOK), BF),
+        jax.ShapeDtypeStruct((FF, DM), BF),
+    )
+    results = pl.pallas_call(
         kernel,
-        out_shape=(
-            jax.ShapeDtypeStruct((TOK, HALF), BF),
-            jax.ShapeDtypeStruct((FF, TOK), BF),
-            jax.ShapeDtypeStruct((FF, TOK), BF),
-            jax.ShapeDtypeStruct((FF, DM), BF),
-        ),
+        out_shape=shapes,
         in_specs=[anywhere] * 4,
         out_specs=[anywhere] * 4,
         scratch_shapes=[
@@ -454,6 +468,14 @@
         ),
         cost_estimate=pl.CostEstimate(flops=flops, bytes_accessed=2**24, transcendentals=0),
     )(gate_pre.T, up_pre.T, w_down, cotangent)
+    layer_out, grad_gate, grad_up, grad_down = pl.pallas_call(
+        place_outputs,
+        out_shape=shapes,
+        in_specs=[anywhere] * 4,
+        out_specs=[anywhere] * 4,
+        scratch_shapes=[pltpu.VMEM(shape.shape, BF) for shape in shapes] + [pltpu.SemaphoreType.DMA((8,))],
+        compiler_params=pltpu.CompilerParams(vmem_limit_bytes=64 * 2**20),
+    )(*results)
     return layer_out, grad_gate.T, grad_up.T, grad_down
 
 

time: 165 us -> 140 us (0.85)
  the two profiles are of different devices: /device:TPU:34 before, /device:TPU:1 now
where the time goes in v3:
time: 140 us; the launch traced here: 137 us
  Pallas kernels  136 us (97%)
    pallas_call x1, Pallas kernels, shards(): pl.pallas_call(kernel, out_shape=shapes, in_specs=[anywhere] * 4, out_spe...  132 us
    pallas_call x1, Pallas kernels, shards(): pl.pallas_call(place_outputs, out_shape=shapes, in_specs=[anywhere] * 4,...  4.09 us

profile of v3, /device:TPU:1, one launch (start us, length us, event | category | flops | bytes accessed | tf_op | source)
XLA Modules:
  0.0 137.2 jit_solution(17674346104370691786)
XLA Ops:
  0.6 132.3 %shard_map.75 = (bf16[512,512]{1,0:T(8,128)(2,1)}, bf16[928,512]{1,0:T(8,128)(2,1)}, bf16[928,512]{1,0:T(8,128)(2,1)}, bf16[928,1024]{1,0:T(8,128)(2,1)}) custom-call(bf16[928,512]{1,0:T(8,128)(2,1)} %bitcast.4, bf16[928,512]{1,0:T(8,128)(2,1)} %bitcast.5, bf16[928,1024]{1,0:T(8,128)(2,1)} %w_in.1, bf16[512,512]{1,0:T(8,128)(2,1)} %cot_in.1), custom_call_target="tpu_custom_call" | custom-call | flops 23353884672 | bytes 16777216 | tf_op jit(solution)/shard_map/pallas_call | solution.py:428
  133.0 4.1 %shard_map.76 = (bf16[512,512]{1,0:T(8,128)(2,1)}, bf16[928,512]{1,0:T(8,128)(2,1)}, bf16[928,512]{1,0:T(8,128)(2,1)}, bf16[928,1024]{1,0:T(8,128)(2,1)}) custom-call(bf16[512,512]{1,0:T(8,128)(2,1)} %get-tuple-element.12.refs_0_, bf16[928,512]{1,0:T(8,128)(2,1)} %get-tuple-element.13.refs_1_, bf16[928,512]{1,0:T(8,128)(2,1)} %get-tuple-element.14.refs_2_, ...), custom_call_target="tpu_custom_call" | custom-call | tf_op jit(solution)/shard_map/pallas_call | solution.py:471

commit v4 on v3

--- a/solution.py
+++ b/solution.py
@@ -13,6 +13,7 @@
 FF = 928
 DM = 1024
 HALF = 512
+SIDE = 96
 CUT = 464
 C = 2
 RC = HALF // C
@@ -120,15 +121,9 @@
     for other in greeted:
         pl.semaphore_signal(barrier, inc=1, device_id=other, device_id_type=MESH)
     loads = []
-    for n, (src, dst) in enumerate(((cot_in, cot), (gate_in, gate), (up_in, up), (w_in, w))):
+    for n, (src, dst) in enumerate(((gate_in, gate), (up_in, up), (cot_in, cot), (w_in, w))):
         loads.append(pltpu.make_async_copy(src, dst, in_sem.at[n]))
         loads[-1].start()
-
-    loads[0].wait()
-    for r in range(0, HALF, 128):
-        OWN[:, r : r + 128] = cot[r : r + 128, :].astype(F32).T.astype(BF)
-    loads[1].wait()
-    loads[2].wait()
 
     def make_hidden(k, _):
         rows = pl.ds(pl.multiple_of(k * 32, 32), 32)
@@ -136,9 +131,17 @@
         HT[dp, rows, :] = (g * jax.nn.sigmoid(g) * up[rows, :].astype(F32)).astype(BF)
         return 0
 
+    loads[0].wait()
+    loads[1].wait()
+    lax.fori_loop(0, 29, make_hidden, 0)
+    loads[2].wait()
+    for r in range(0, HALF, 128):
+        OWN[:, r : r + 128] = cot[r : r + 128, :].astype(F32).T.astype(BF)
+
     pl.semaphore_wait(barrier, len(greeted))
     cp = Copies(send_sem, recv_sem)
     low, high = pl.ds(0, CUT), pl.ds(CUT, FF - CUT)
+    most, side = pl.ds(0, FF - SIDE), pl.ds(FF - SIDE, SIDE)
 
     def crow(k, size=RC):
         return pl.ds(pl.multiple_of(c * HALF + k, 16), size)
@@ -150,7 +153,6 @@
     for k in range(C):
         at = pl.ds(k * RC, RC)
         t1.append(cp.put_or_keep(here(T1[k]), OWN.at[at], ZM.at[at], T1[k], ZM.at[at]))
-    lax.fori_loop(0, 29, make_hidden, 0)
     s1p, s1m = [share(HT.at[dp, low], X(1))], [share(HT.at[dp, high], X(-1))]
     s1y = share(HT.at[dp], YL)
 
@@ -203,7 +205,7 @@
         near[False, k] = spread(False, k)
         cross(0, False, k)
     s1y.wait_recv()
-    par = HT.at[tok(0, True)]
+    par = HT.at[tok(0, True), most]
     s3p, s3m = share(par, X(1)), share(par, X(-1))
 
     for k in range(C):
@@ -226,6 +228,7 @@
             cross(-1, row, k)
     s1p[1].wait_recv()
     s1m[1].wait_recv()
+    s6 = [share(HT.at[tok(dx, False), side], YL) for dx in (1, -1)]
     lx.append(make_layer(tok(1, False)))
     lx.append(make_layer(tok(-1, False)))
     for row in (False, True):
@@ -247,14 +250,17 @@
     make_grad(tok(2, True))
     g1 = cp.put(G.at[tok(2, True)], R1, YL)
     make_grad(tok(1, True))
-    g3p = cp.put(G.at[tok(1, True)], R3.at[0], X(1))
+    g3p = cp.put(G.at[tok(1, True), most], R3.at[0, most], X(1))
     make_grad(tok(-1, True))
-    g3m = cp.put(G.at[tok(-1, True)], R3.at[1], X(-1))
+    g3m = cp.put(G.at[tok(-1, True), most], R3.at[1, most], X(-1))
+    g6 = [cp.put(G.at[tok(dx, True), side], R3.at[n, side], YL) for n, dx in enumerate((1, -1))]
     s4.wait_recv()
     lx.append(make_layer(tok(2, True)))
     s3p.wait_recv()
+    s6[1].wait_recv()
     lx.append(make_layer(tok(-1, True)))
     s3m.wait_recv()
+    s6[0].wait_recv()
     lx.append(make_layer(tok(1, True)))
     for f in lx:
         f.wait_recv()
@@ -317,6 +323,9 @@
     g2a = cp.put(G.at[two, low], RAB.at[low], X(1))
     g2b = cp.put(G.at[two, high], RAB.at[high], X(-1))
     up_one, down_one = tok(1, False), tok(-1, False)
+    for n, block in enumerate((up_one, down_one)):
+        g6[n].wait_recv()
+        G[block, side] = (G[block, side].astype(F32) + R3[n, side].astype(F32)).astype(BF)
     g5 = [cp.put(G.at[up_one, high], RO.at[0, high], X(1)), cp.put(G.at[down_one, low], RO.at[1, low], X(-1))]
     for k in range(C):
         pair(0, True, k)
@@ -338,9 +347,21 @@
     g3p.wait_recv()
     g3m.wait_recv()
     par = tok(0, True)
-    G[par] = (G[par].astype(F32) + R3[0].astype(F32) + R3[1].astype(F32)).astype(BF)
+    G[par, most] = (G[par, most].astype(F32) + R3[0, most].astype(F32) + R3[1, most].astype(F32)).astype(BF)
     g5.append(cp.put(G.at[par], RO.at[2], YL))
 
+    g2a.wait_recv()
+    G[up_one, low] = (G[up_one, low].astype(F32) + RAB[low].astype(F32)).astype(BF)
+    g2b.wait_recv()
+    G[down_one, high] = (G[down_one, high].astype(F32) + RAB[high].astype(F32)).astype(BF)
+
+    def last(part):
+        at = pl.ds(*((0, 256) if part == 0 else (256, CUT - 256)))
+        g5.append(cp.put(G.at[up_one, at], RO.at[0, at], X(1)))
+        at = pl.ds(*((CUT, 256) if part == 0 else (CUT + 256, FF - CUT - 256)))
+        g5.append(cp.put(G.at[down_one, at], RO.at[1, at], X(-1)))
+
+    last(0)
     outs.append(weight_grad(0))
     outs.append(weight_grad(1))
 
@@ -355,13 +376,7 @@
         ).astype(BF)
         sw.append(cp.put_or_keep(here(SW[k]), FIN.at[at], SWP.at[at], SW[k], SWP.at[at]))
 
-    g2a.wait_recv()
-    G[up_one, low] = (G[up_one, low].astype(F32) + RAB[low].astype(F32)).astype(BF)
-    g5.append(cp.put(G.at[up_one, low], RO.at[0, low], X(1)))
-    g2b.wait_recv()
-    G[down_one, high] = (G[down_one, high].astype(F32) + RAB[high].astype(F32)).astype(BF)
-    g5.append(cp.put(G.at[down_one, high], RO.at[1, high], X(-1)))
-
+    last(1)
     outs[0].wait()
     outs.append(weight_grad(2))
     outs[1].wait()
@@ -376,14 +391,11 @@
     copy.start()
     outs.append(copy)
 
-    for f in g5:
-        f.wait_recv()
-
     def finish(k, _):
-        rows = pl.ds(pl.multiple_of(k * 32, 32), 32)
+        rows = pl.ds(pl.multiple_of(k * 16, 16), 16)
         total = G[dp, rows, :].astype(F32)
-        for side in range(3):
-            total = total + RO[side, rows, :].astype(F32)
+        for n in range(3):
+            total = total + RO[n, rows, :].astype(F32)
         g = gate[rows, :].astype(F32)
         squash = jax.nn.sigmoid(g)
         gu_stage[rows, :] = (total * g * squash).astype(BF)
@@ -392,11 +404,18 @@
         ).astype(BF)
         return 0
 
-    lax.fori_loop(0, 29, finish, 0)
-    for n, (stage, out) in enumerate(((gg_stage, gg_out), (gu_stage, gu_out))):
-        copy = pltpu.make_async_copy(stage, out, out_sem.at[5 + n])
-        copy.start()
-        outs.append(copy)
+    n = 5
+    for part, spans in enumerate((((0, 256), (CUT, CUT + 256)), ((256, CUT), (CUT + 256, FF)))):
+        for f in g5[:5] if part == 0 else g5[5:]:
+            f.wait_recv()
+        for start, end in spans:
+            lax.fori_loop(start // 16, end // 16, finish, 0, unroll=2 if part == 0 else 1)
+            for stage, out in ((gg_stage, gg_out), (gu_stage, gu_out)):
+                at = pl.ds(start, end - start)
+                copy = pltpu.make_async_copy(stage.at[at], out.at[at], out_sem.at[n])
+                copy.start()
+                outs.append(copy)
+                n += 1
     cp.finish()
     for copy in outs[2:]:
         copy.wait()
@@ -404,13 +423,18 @@
 
 def place_outputs(*refs):
     sources, results, stages, sems = refs[:4], refs[4:8], refs[8:12], refs[12]
-    arrive = [pltpu.make_async_copy(sources[n], stages[n], sems.at[n]) for n in range(4)]
-    leave = [pltpu.make_async_copy(stages[n], results[n], sems.at[4 + n]) for n in range(4)]
+    arrive, leave = [], []
+    for n in (0, 3, 1, 2):
+        rows = sources[n].shape[0] // 2
+        for part in range(2):
+            at, k = pl.ds(part * rows, rows), len(arrive)
+            arrive.append(pltpu.make_async_copy(sources[n].at[at], stages[n].at[at], sems.at[k]))
+            leave.append(pltpu.make_async_copy(stages[n].at[at], results[n].at[at], sems.at[8 + k]))
     for copy in arrive:
         copy.start()
-    for n in range(4):
-        arrive[n].wait()
-        leave[n].start()
+    for k in range(8):
+        arrive[k].wait()
+        leave[k].start()
     for copy in leave:
         copy.wait()
 
@@ -461,7 +485,7 @@
             pltpu.SemaphoreType.DMA((n_copies,)),
             pltpu.SemaphoreType.DMA((n_copies,)),
             pltpu.SemaphoreType.DMA((4,)),
-            pltpu.SemaphoreType.DMA((7,)),
+            pltpu.SemaphoreType.DMA((13,)),
         ],
         compiler_params=pltpu.CompilerParams(
             collective_id=0, has_side_effects=True, vmem_limit_bytes=64 * 2**20
@@ -473,7 +497,7 @@
         out_shape=shapes,
         in_specs=[anywhere] * 4,
         out_specs=[anywhere] * 4,
-        scratch_shapes=[pltpu.VMEM(shape.shape, BF) for shape in shapes] + [pltpu.SemaphoreType.DMA((8,))],
+        scratch_shapes=[pltpu.VMEM(shape.shape, BF) for shape in shapes] + [pltpu.SemaphoreType.DMA((16,))],
         compiler_params=pltpu.CompilerParams(vmem_limit_bytes=64 * 2**20),
     )(*results)
     return layer_out, grad_gate.T, grad_up.T, grad_down

time: 140 us -> 135 us (0.964)
  Pallas kernels: 136 us -> 133 us
    pallas_call x1, Pallas kernels: 132 us -> 129 us  [shards(): pl.pallas_call(kernel, out_shape=shapes, in_specs=[anywhere] * 4, out_spe...]
where the time goes in v4:
time: 135 us; the launch traced here: 133 us
  Pallas kernels  133 us (99%)
    pallas_call x1, Pallas kernels, shards(): pl.pallas_call(kernel, out_shape=shapes, in_specs=[anywhere] * 4, out_spe...  129 us
    pallas_call x1, Pallas kernels, shards(): pl.pallas_call(place_outputs, out_shape=shapes, in_specs=[anywhere] * 4,...  3.57 us

profile of v4, /device:TPU:1, one launch (start us, length us, event | category | flops | bytes accessed | tf_op | source)
XLA Modules:
  0.0 133.4 jit_solution(13539085688150901062)
XLA Ops:
  0.6 129.0 %shard_map.75 = (bf16[512,512]{1,0:T(8,128)(2,1)}, bf16[928,512]{1,0:T(8,128)(2,1)}, bf16[928,512]{1,0:T(8,128)(2,1)}, bf16[928,1024]{1,0:T(8,128)(2,1)}) custom-call(bf16[928,512]{1,0:T(8,128)(2,1)} %bitcast.4, bf16[928,512]{1,0:T(8,128)(2,1)} %bitcast.5, bf16[928,1024]{1,0:T(8,128)(2,1)} %w_in.1, bf16[512,512]{1,0:T(8,128)(2,1)} %cot_in.1), custom_call_target="tpu_custom_call" | custom-call | flops 23353884672 | bytes 16777216 | tf_op jit(solution)/shard_map/pallas_call | solution.py:452
  129.6 3.6 %shard_map.76 = (bf16[512,512]{1,0:T(8,128)(2,1)}, bf16[928,512]{1,0:T(8,128)(2,1)}, bf16[928,512]{1,0:T(8,128)(2,1)}, bf16[928,1024]{1,0:T(8,128)(2,1)}) custom-call(bf16[512,512]{1,0:T(8,128)(2,1)} %get-tuple-element.12.refs_0_, bf16[928,512]{1,0:T(8,128)(2,1)} %get-tuple-element.13.refs_1_, bf16[928,512]{1,0:T(8,128)(2,1)} %get-tuple-element.14.refs_2_, ...), custom_call_target="tpu_custom_call" | custom-call | tf_op jit(solution)/shard_map/pallas_call | solution.py:495

commit v5 on v0

v5 whole, which is shorter than its diff:
```python
import jax
import jax.numpy as jnp
from jax import lax
from jax.experimental import pallas as pl
from jax.experimental.pallas import tpu as pltpu
from jax.sharding import PartitionSpec as P

MESH = pl.DeviceIdType.MESH
BF = jnp.bfloat16
F32 = jnp.float32

TOK = 512
FF = 928
DM = 1024
HALF = 512
CUT = 464
C = 4
RC = HALF // C
HC = RC // 2
CL = 2
RL = HALF // CL
HL = RL // 2


class Copies:
    def __init__(self, send, recv):
        self.send, self.recv, self.all, self.n = send, recv, [], 0

    def ids(self, count):
        self.n += count
        return self.n - count

    def put(self, src, dst, target):
        k = self.ids(1)
        copy = pltpu.make_async_remote_copy(
            src, dst, self.send.at[k], self.recv.at[k], device_id=target, device_id_type=MESH
        )
        copy.start()
        self.all.append((None, copy))
        return copy

    def put_or_keep(self, keep, src, dst, target, at=None):
        ks, kr = at or (self.ids(1),) * 2
        copy = pltpu.make_async_remote_copy(
            src, dst, self.send.at[ks], self.recv.at[kr], device_id=target, device_id_type=MESH
        )
        pl.when(keep)(pltpu.make_async_copy(src, dst, self.recv.at[kr]).start)
        pl.when(jnp.logical_not(keep))(copy.start)
        self.all.append((keep, copy))
        return ks, kr

    def landed(self, keep, src, landing, kr, target):
        got = pltpu.make_async_remote_copy(
            src, landing, self.send.at[kr], self.recv.at[kr], device_id=target, device_id_type=MESH
        )
        pl.when(keep)(pltpu.make_async_copy(src, landing, self.recv.at[kr]).wait)
        pl.when(jnp.logical_not(keep))(got.wait_recv)

    def finish(self):
        for keep, copy in self.all:
            if keep is None:
                copy.wait_send()
            else:
                pl.when(jnp.logical_not(keep))(copy.wait_send)
        self.all = []


def nn(a, b):
    return lax.dot_general(a, b, (((1,), (0,)), ((), ())), preferred_element_type=F32)


def nt(a, b):
    return lax.dot_general(a, b, (((1,), (1,)), ((), ())), preferred_element_type=F32)


def kernel(
    gate_in, up_in, w_in, cot_in, lay_out, gg_out, gu_out, gd_out,
    gate, up, cot, W2, WT, HT, CT, OWN, ZM, G, RAB, RO, LO, LS, LX, LH, LD, BX, BY, FIN, SWP,
    acc, GDS, GDR, gd_stage, lay_stage, gg_stage, gu_stage, send_sem, recv_sem, in_sem, out_sem,
):
    dp, t = lax.axis_index("dp"), lax.axis_index("tensor")
    x, yl = dp // 2, dp % 2
    yh, z, c = t // 8, (t // 2) % 4, t % 2
    x1, x0, z1, z0 = x // 2, x % 2, z // 2, z % 2

    def X(d):
        return (((x + d + 4) % 4) * 2 + yl, t)

    def Z(d):
        return (dp, yh * 8 + ((z + d + 4) % 4) * 2 + c)

    YL = (x * 2 + 1 - yl, t)
    YH = (dp, (1 - yh) * 8 + z * 2 + c)
    CORE = (dp, t + 1 - 2 * c)
    T1 = (dp, yh * 8 + (2 * z0 + (x0 + z1) % 2) * 2 + c)
    T1S = (dp, yh * 8 + (2 * ((x0 + z0) % 2) + z1) * 2 + c)
    hz = (x0 + z0) % 2
    t1_keep = T1[1] == t

    def owner(b):
        return ((2 * b + hz) * 2 + yl, t)

    def tok(dx):
        return (x + dx + 4) % 4

    def place(dz, b):
        at = (z + dz + 4) % 4
        return 2 * b + (x0 + at) % 2, at // 2

    barrier = pltpu.get_barrier_semaphore()
    greeted = (X(1), X(-1), YL, Z(1), Z(-1), YH, CORE, T1, T1S, owner(0), owner(1))
    for other in greeted:
        pl.semaphore_signal(barrier, inc=1, device_id=other, device_id_type=MESH)
    loads = []
    for n, (src, dst) in enumerate(((w_in, W2.at[yl]), (gate_in, gate), (up_in, up), (cot_in, cot))):
        loads.append(pltpu.make_async_copy(src, dst, in_sem.at[n]))
        loads[-1].start()

    def make_hidden(k, _):
        rows = pl.ds(pl.multiple_of(k * 32, 32), 32)
        g = gate[rows, :].astype(F32)
        HT[x, rows, :] = (g * jax.nn.sigmoid(g) * up[rows, :].astype(F32)).astype(BF)
        return 0

    loads[3].wait()
    for r in range(0, HALF, 128):
        OWN[:, r : r + 128] = cot[r : r + 128, :].astype(F32).T.astype(BF)
    loads[0].wait()
    loads[1].wait()
    loads[2].wait()
    lax.fori_loop(0, 29, make_hidden, 0)

    pl.semaphore_wait(barrier, len(greeted))
    cp = Copies(send_sem, recv_sem)
    low, high = pl.ds(0, CUT), pl.ds(CUT, FF - CUT)

    def crow(k, size=RC):
        return pl.ds(pl.multiple_of(c * HALF + k, 16), size)

    def share(ref, target):
        return cp.put(ref, ref, target)

    t1 = []
    for k in range(C):
        at = pl.ds(k * RC, RC)
        t1.append(cp.put_or_keep(t1_keep, OWN.at[at], ZM.at[0, at], T1)[1])

    def send_w(start, size):
        return share(W2.at[yl, :, pl.ds(start, size)], YL)

    ws = [send_w(0, 128)]
    a0, a1 = pl.ds(0, 240), pl.ds(FF - 240, 240)
    s1p, s1m = [share(HT.at[x, a0], X(1))], [share(HT.at[x, a1], X(-1))]

    def turn(s, n):
        WT[s, pl.ds(n * 256, 256), :] = W2[s, :, pl.ds(n * 256, 256)].astype(F32).T.astype(BF)

    t2_at = [cp.ids(2) for _ in range(C)]

    def send_t2(n, k):
        b = (n + yh) % 2
        at = pl.ds(k * RC, RC)
        cp.put_or_keep(
            2 * b + hz == x, ZM.at[n, at], CT.at[2 * x + z1, crow(k * RC)], owner(b), (t2_at[k] + n, t2_at[k] + x1)
        )

    def spread(b, k):
        token, s = place(0, b)
        ref = CT.at[2 * token + s, crow(k * RC)]
        return share(ref, Z(1)), share(ref, Z(-1))

    def forward(b, k):
        token, s = place(-1, b)
        lower = CT.at[2 * token + s, crow(k * RC, HC)]
        token, s = place(1, b)
        upper = CT.at[2 * token + s, crow(k * RC + HC, HC)]
        return share(lower, Z(1)), share(upper, Z(-1))

    t5, near, far = [], {}, {}

    def cross(dz, b):
        token, s = place(dz, b)
        t5.append(share(CT.at[2 * token + s, crow(0, HALF)], CORE))

    def owned(k):
        for b in range(2):
            landing = CT.at[2 * (2 * b + hz) + z1, crow(k * RC)]
            cp.landed(2 * b + hz == x, ZM.at[0, pl.ds(k * RC, RC)], landing, t2_at[k] + b, owner(b))
            near[b, k] = spread(b, k)

    t3 = []
    for k in range(C):
        at = pl.ds(k * RC, RC)
        cp.landed(t1_keep, OWN.at[at], ZM.at[0, at], t1[k], T1)
        t3.append(cp.put(ZM.at[0, at], ZM.at[1, at], YH))
        send_t2(0, k)
        if k > 0:
            t3[k - 1].wait_recv()
            send_t2(1, k - 1)
    owned(0)
    t3[-1].wait_recv()
    send_t2(1, C - 1)
    a0b, a1b = pl.ds(240, CUT - 240), pl.ds(CUT, FF - 240 - CUT)
    s1p.append(share(HT.at[x, a0b], X(1)))
    s1m.append(share(HT.at[x, a1b], X(-1)))
    for start, size in ((128, 128), (512, 256), (256, 256), (768, 256)):
        ws.append(send_w(start, size))
    s1p.append(share(HT.at[x, high], X(1)))
    s1m.append(share(HT.at[x, low], X(-1)))

    for k in range(1, C):
        owned(k)
    for n in range(4):
        turn(yl, n)

    def make_layer(s, k, first, step, count):
        def part(n, _):
            g, cols = (x + first + step * (n // 2)) % 4, pl.ds(pl.multiple_of((n % 2) * 256, 256), 256)
            there = pl.ds(pl.multiple_of((1 - c) * HALF + k * RL, RL), RL)
            here = pl.ds(pl.multiple_of(c * HALF + k * RL, RL), RL)
            h = HT[g, :, cols]
            LS[s, k, g, :, cols] = nn(WT[s, there, :], h).astype(BF)
            LO[s, k, g, :, cols] = nn(WT[s, here, :], h).astype(BF)
            return 0

        lax.fori_loop(0, 2 * count, part, 0)

    def cross_layer(s, k):
        return cp.put(LS.at[s, k], LX.at[s, k], CORE)

    cross(0, 0)
    cross(0, 1)
    s1p[0].wait_recv()
    s1m[0].wait_recv()
    s2 = [share(HT.at[tok(-1), a0], X(1)), share(HT.at[tok(1), a1], X(-1))]
    make_layer(yl, 0, 0, 1, 1)
    make_layer(yl, 1, 0, 1, 1)
    s1p[1].wait_recv()
    s1m[1].wait_recv()
    s2 += [share(HT.at[tok(-1), a0b], X(1)), share(HT.at[tok(1), a1b], X(-1))]

    for k in range(C):
        for b in range(2):
            near[b, k][0].wait_recv()
            near[b, k][1].wait_recv()
            far[b, k] = forward(b, k)
    for b in range(2):
        cross(1, b)
        cross(-1, b)
    s1p[2].wait_recv()
    s1m[2].wait_recv()
    make_layer(yl, 0, 1, 2, 2)
    make_layer(yl, 1, 1, 2, 2)
    for w in ws[:3]:
        w.wait_recv()
    turn(1 - yl, 0)
    turn(1 - yl, 2)
    make_layer(1 - yl, 0, 0, 1, 2)
    make_layer(1 - yl, 0, 3, 1, 1)
    for f in s2:
        f.wait_recv()
    make_layer(yl, 0, 2, 1, 1)
    lx = {0: cross_layer(yl, 0)}
    make_layer(1 - yl, 0, 2, 1, 1)
    lx[1] = cross_layer(1 - yl, 0)
    for b in range(2):
        for k in range(C):
            far[b, k][0].wait_recv()
            far[b, k][1].wait_recv()
        cross(2, b)

    def weight_sum(s, n):
        cols = pl.ds(n * 256, 256)
        acc[...] = jnp.zeros_like(acc)

        def add(g, _):
            acc[...] += nt(HT[g], CT[2 * g + s, cols, :])
            return 0

        lax.fori_loop(0, 4, add, 0)

    gd = {}

    def partner_sum(n):
        weight_sum(1 - yl, n)
        GDS[n] = acc[...].astype(BF)

    def send_sum(n, start=0, size=FF):
        at = pl.ds(start, size)
        gd.setdefault(n, []).append(cp.put(GDS.at[n, at], GDR.at[n, at], YL))

    def make_grad(g):
        def part(k, _):
            cols = pl.ds(pl.multiple_of(k * 256, 256), 256)
            G[g, :, cols] = (nn(W2[0], CT[2 * g, :, cols]) + nn(W2[1], CT[2 * g + 1, :, cols])).astype(BF)
            return 0

        lax.fori_loop(0, 2, part, 0)

    def pair(dz, b, k):
        token, s = place(dz, b)
        LO[s, k, token] = (LO[s, k, token].astype(F32) + LX[s, k, token].astype(F32)).astype(BF)

    halves, directs = {}, {}

    def begin(k):
        for b in range(2):
            pair(2, b, k)
            token, s = place(2, b)
            halves[b, k] = (
                cp.put(LO.at[s, k, token, pl.ds(0, HL)], LH.at[b, 0, k], Z(1)),
                cp.put(LO.at[s, k, token, pl.ds(HL, HL)], LH.at[b, 1, k], Z(-1)),
            )
        for b in range(2):
            pair(1, b, k)
            pair(-1, b, k)

    def relay(b, k):
        sent = []
        for side, dz in ((0, 1), (1, -1)):
            token, s = place(dz, b)
            halves[b, k][side].wait_recv()
            at = pl.ds(side * HL, HL)
            LO[s, k, token, at] = (LO[s, k, token, at].astype(F32) + LH[b, side, k].astype(F32)).astype(BF)
            sent.append(cp.put(LO.at[s, k, token], LD.at[b, side, k], Z(dz)))
        directs[b, k] = sent

    back_at = [cp.ids(2) for _ in range(CL)]

    def send_back(b, k):
        token, s = place(0, b)
        directs[b, k][0].wait_recv()
        directs[b, k][1].wait_recv()
        LO[s, k, token] = (
            LO[s, k, token].astype(F32) + LD[b, 0, k].astype(F32) + LD[b, 1, k].astype(F32)
        ).astype(BF)
        cp.put_or_keep(token == x, LO.at[s, k, token], BX.at[x1, k], owner(b), (back_at[k] + b, back_at[k] + x1))

    lx[0].wait_recv()
    lx[1].wait_recv()
    begin(0)
    for f in t5:
        f.wait_recv()
    partner_sum(0)
    send_sum(0)
    make_layer(yl, 1, 2, 1, 1)
    lx[2] = cross_layer(yl, 1)
    ws[3].wait_recv()
    ws[4].wait_recv()
    turn(1 - yl, 1)
    turn(1 - yl, 3)
    make_layer(1 - yl, 1, 0, 1, 4)
    lx[3] = cross_layer(1 - yl, 1)
    relay(0, 0)
    relay(1, 0)
    make_grad(tok(2))
    g2a = cp.put(G.at[tok(2), low], RAB.at[low], X(1))
    g2b = cp.put(G.at[tok(2), high], RAB.at[high], X(-1))
    partner_sum(1)
    send_sum(1)
    lx[2].wait_recv()
    lx[3].wait_recv()
    begin(1)
    for k in range(CL):
        pair(0, 0, k)
        pair(0, 1, k)
    up_one, down_one = tok(1), tok(-1)
    make_grad(up_one)
    partner_sum(2)
    send_sum(2)
    send_back(0, 0)
    send_back(1, 0)
    g5 = [cp.put(G.at[up_one, high], RO.at[0, high], X(1))]
    make_grad(down_one)
    g5.append(cp.put(G.at[down_one, low], RO.at[1, low], X(-1)))
    relay(0, 1)
    relay(1, 1)
    partner_sum(3)

    ly = []

    def meet(k):
        for r in range(2):
            cp.landed(2 * r + hz == x, LO.at[0, 0, 0], BX.at[r, k], back_at[k] + r, owner(r))
        ly.append(cp.put(BX.at[1 - yh, k], BY.at[k], YH))

    meet(0)
    send_sum(3, 0, CUT)
    g2a.wait_recv()
    G[up_one, low] = (G[up_one, low].astype(F32) + RAB[low].astype(F32)).astype(BF)
    g2b.wait_recv()
    G[down_one, high] = (G[down_one, high].astype(F32) + RAB[high].astype(F32)).astype(BF)
    send_back(0, 1)
    send_back(1, 1)
    g5.append(cp.put(G.at[up_one, low], RO.at[0, low], X(1)))
    g5.append(cp.put(G.at[down_one, high], RO.at[1, high], X(-1)))
    make_grad(x)

    sw = []

    def home(k):
        ly[k].wait_recv()
        at = pl.ds(k * RL, RL)
        FIN[at] = (BX[yh, k].astype(F32) + BY[k].astype(F32)).astype(BF)
        sw.append(cp.put_or_keep(t1_keep, FIN.at[at], SWP.at[at], T1S)[1])

    outs = []

    def own_sum(n):
        weight_sum(yl, n)
        for f in gd[n]:
            f.wait_recv()
        if n > 1:
            outs[n - 2].wait()
        gd_stage[n % 2] = (acc[...] + GDR[n].astype(F32)).astype(BF)
        copy = pltpu.make_async_copy(gd_stage.at[n % 2], gd_out.at[:, pl.ds(n * 256, 256)], out_sem.at[n])
        copy.start()
        outs.append(copy)

    own_sum(0)
    meet(1)
    send_sum(3, CUT, FF - CUT)
    home(0)
    own_sum(1)
    home(1)

    for f in g5:
        f.wait_recv()

    def finish(k, _):
        rows = pl.ds(pl.multiple_of(k * 32, 32), 32)
        total = G[x, rows, :].astype(F32) + RO[0, rows, :].astype(F32) + RO[1, rows, :].astype(F32)
        g = gate[rows, :].astype(F32)
        squash = jax.nn.sigmoid(g)
        gu_stage[rows, :] = (total * g * squash).astype(BF)
        gg_stage[rows, :] = (
            total * up[rows, :].astype(F32) * squash * (1.0 + g * (1.0 - squash))
        ).astype(BF)
        return 0

    lax.fori_loop(0, 29, finish, 0)
    for n, (stage, out) in enumerate(((gg_stage, gg_out), (gu_stage, gu_out))):
        copy = pltpu.make_async_copy(stage, out, out_sem.at[5 + n])
        copy.start()
        outs.append(copy)
    weight_sum(yl, 2)
    gd[2][0].wait_recv()
    outs[0].wait()
    gd_stage[0] = (acc[...] + GDR[2].astype(F32)).astype(BF)
    third = pltpu.make_async_copy(gd_stage.at[0], gd_out.at[:, pl.ds(512, 256)], out_sem.at[2])
    third.start()
    weight_sum(yl, 3)

    for k in range(CL):
        at = pl.ds(k * RL, RL)
        cp.landed(t1_keep, FIN.at[at], SWP.at[at], sw[k], T1S)
        for r in range(0, TOK, 128):
            lay_stage[r : r + 128, k * RL : (k + 1) * RL] = SWP[at, r : r + 128].astype(F32).T.astype(BF)
    lay = pltpu.make_async_copy(lay_stage, lay_out, out_sem.at[4])
    lay.start()
    cp.finish()
    outs[1].wait()
    gd[3][0].wait_recv()
    gd[3][1].wait_recv()
    gd_stage[1] = (acc[...] + GDR[3].astype(F32)).astype(BF)
    fourth = pltpu.make_async_copy(gd_stage.at[1], gd_out.at[:, pl.ds(768, 256)], out_sem.at[3])
    fourth.start()
    for copy in (outs[2], outs[3], third, lay, fourth):
        copy.wait()


def place_outputs(*refs):
    sources, results, stages, sems = refs[:4], refs[4:8], refs[8:12], refs[12]
    arrive, leave = [], []
    for n in (0, 3, 1, 2):
        rows = sources[n].shape[0] // 2
        for part in range(2):
            at, k = pl.ds(part * rows, rows), len(arrive)
            arrive.append(pltpu.make_async_copy(sources[n].at[at], stages[n].at[at], sems.at[k]))
            leave.append(pltpu.make_async_copy(stages[n].at[at], results[n].at[at], sems.at[8 + k]))
    for copy in arrive:
        copy.start()
    for k in range(8):
        arrive[k].wait()
        leave[k].start()
    for copy in leave:
        copy.wait()


def shards(gate_pre, up_pre, w_down, cotangent):
    anywhere = pl.BlockSpec(memory_space=pl.ANY)
    n_copies = 140
    flops = 2 * 3 * TOK * FF * 8192
    shapes = (
        jax.ShapeDtypeStruct((TOK, HALF), BF),
        jax.ShapeDtypeStruct((FF, TOK), BF),
        jax.ShapeDtypeStruct((FF, TOK), BF),
        jax.ShapeDtypeStruct((FF, DM), BF),
    )
    results = pl.pallas_call(
        kernel,
        out_shape=shapes,
        in_specs=[anywhere] * 4,
        out_specs=[anywhere] * 4,
        scratch_shapes=[
            pltpu.VMEM((FF, TOK), BF),
            pltpu.VMEM((FF, TOK), BF),
            pltpu.VMEM((TOK, HALF), BF),
            pltpu.VMEM((2, FF, DM), BF),
            pltpu.VMEM((2, DM, FF), BF),
            pltpu.VMEM((4, FF, TOK), BF),
            pltpu.VMEM((8, DM, TOK), BF),
            pltpu.VMEM((HALF, TOK), BF),
            pltpu.VMEM((2, HALF, TOK), BF),
            pltpu.VMEM((4, FF, TOK), BF),
            pltpu.VMEM((FF, TOK), BF),
            pltpu.VMEM((2, FF, TOK), BF),
            pltpu.VMEM((2, CL, 4, RL, TOK), BF),
            pltpu.VMEM((2, CL, 4, RL, TOK), BF),
            pltpu.VMEM((2, CL, 4, RL, TOK), BF),
            pltpu.VMEM((2, 2, CL, HL, TOK), BF),
            pltpu.VMEM((2, 2, CL, RL, TOK), BF),
            pltpu.VMEM((2, CL, RL, TOK), BF),
            pltpu.VMEM((CL, RL, TOK), BF),
            pltpu.VMEM((HALF, TOK), BF),
            pltpu.VMEM((HALF, TOK), BF),
            pltpu.VMEM((FF, 256), F32),
            pltpu.VMEM((4, FF, 256), BF),
            pltpu.VMEM((4, FF, 256), BF),
            pltpu.VMEM((2, FF, 256), BF),
            pltpu.VMEM((TOK, HALF), BF),
            pltpu.VMEM((FF, TOK), BF),
            pltpu.VMEM((FF, TOK), BF),
            pltpu.SemaphoreType.DMA((n_copies,)),
            pltpu.SemaphoreType.DMA((n_copies,)),
            pltpu.SemaphoreType.DMA((4,)),
            pltpu.SemaphoreType.DMA((7,)),
        ],
        compiler_params=pltpu.CompilerParams(
            collective_id=0, has_side_effects=True, vmem_limit_bytes=64 * 2**20
        ),
        cost_estimate=pl.CostEstimate(flops=flops, bytes_accessed=2**24, transcendentals=0),
    )(gate_pre.T, up_pre.T, w_down, cotangent)
    layer_out, grad_gate, grad_up, grad_down = pl.pallas_call(
        place_outputs,
        out_shape=shapes,
        in_specs=[anywhere] * 4,
        out_specs=[anywhere] * 4,
        scratch_shapes=[pltpu.VMEM(shape.shape, BF) for shape in shapes] + [pltpu.SemaphoreType.DMA((16,))],
        compiler_params=pltpu.CompilerParams(vmem_limit_bytes=64 * 2**20),
    )(*results)
    return layer_out, grad_gate.T, grad_up.T, grad_down


def solution(mesh):
    placed = (P("dp", "tensor"), P("dp", "tensor"), P("tensor", "dp"), P("dp", "tensor"))
    return jax.shard_map(
        shards,
        mesh=mesh,
        in_specs=placed,
        out_specs=(P("dp", "tensor"), P("dp", "tensor"), P("dp", "tensor"), P("tensor", "dp")),
        check_vma=False,
    )
```

time: 800 us -> 132 us (0.17)
  waiting for transfers between devices: 737 us -> 0 us
  Pallas kernels: 0 us -> 131 us
  matrix products: 48.8 us -> 0 us
  between operations: 13.8 us -> 0.8 us
    reduce_scatter x2 -> x0, waiting for transfers between devices: 371 us -> none  [the longest x1 300 us: shards(): lax.psum_scatter(lax.dot_general(full_cot, hidden, (((0,), (0,)), ((), ()...]
    all_gather x2 -> x0, waiting for transfers between devices: 364 us -> none  [the longest x1 300 us: shards(): full_weight = lax.all_gather(w_down, 'dp', axis=1, tiled=True)]
    pallas_call x0 -> x2, Pallas kernels: none -> 131 us  [the longest x1 127 us: shards(): pl.pallas_call(kernel, out_shape=shapes, in_specs=[anywhere] * 4, out_spe...]
    dot_general x3 -> x0, matrix products: 48.8 us -> none  [the longest x1 16.8 us: shards(): lax.dot_general(full_cot, full_weight, (((1,), (1,)), ((), ())), preferre...]
  transfers between devices with their start and end apart: 4 -> 0, of which waited for: 4 -> 0; matrix products, arithmetic and copies ran while one was open for 6% -> 0% of each run, Pallas kernels for 0% -> 0%
where the time goes in v5:
time: 132 us
  Pallas kernels  131 us (99%)
    pallas_call x1, Pallas kernels, shards(): pl.pallas_call(kernel, out_shape=shapes, in_specs=[anywhere] * 4, out_spe...  127 us
    pallas_call x1, Pallas kernels, shards(): pl.pallas_call(place_outputs, out_shape=shapes, in_specs=[anywhere] * 4,...  3.57 us

profile of v5, /device:TPU:1, one launch (start us, length us, event | category | flops | bytes accessed | tf_op | source)
XLA Modules:
  0.0 131.8 jit_solution(4615284238883464462)
XLA Ops:
  0.6 127.4 %shard_map.75 = (bf16[512,512]{1,0:T(8,128)(2,1)}, bf16[928,512]{1,0:T(8,128)(2,1)}, bf16[928,512]{1,0:T(8,128)(2,1)}, bf16[928,1024]{1,0:T(8,128)(2,1)}) custom-call(bf16[928,512]{1,0:T(8,128)(2,1)} %bitcast.4, bf16[928,512]{1,0:T(8,128)(2,1)} %bitcast.5, bf16[928,1024]{1,0:T(8,128)(2,1)} %w_in.1, bf16[512,512]{1,0:T(8,128)(2,1)} %cot_in.1), custom_call_target="tpu_custom_call" | custom-call | flops 23353884672 | bytes 16777216 | tf_op jit(solution)/shard_map/pallas_call | solution.py:500
  128.1 3.6 %shard_map.76 = (bf16[512,512]{1,0:T(8,128)(2,1)}, bf16[928,512]{1,0:T(8,128)(2,1)}, bf16[928,512]{1,0:T(8,128)(2,1)}, bf16[928,1024]{1,0:T(8,128)(2,1)}) custom-call(bf16[512,512]{1,0:T(8,128)(2,1)} %get-tuple-element.12.refs_0_, bf16[928,512]{1,0:T(8,128)(2,1)} %get-tuple-element.13.refs_1_, bf16[928,512]{1,0:T(8,128)(2,1)} %get-tuple-element.14.refs_2_, ...), custom_call_target="tpu_custom_call" | custom-call | tf_op jit(solution)/shard_map/pallas_call | solution.py:544

commit v6 on v5

--- a/solution.py
+++ b/solution.py
@@ -112,7 +112,7 @@
     for other in greeted:
         pl.semaphore_signal(barrier, inc=1, device_id=other, device_id_type=MESH)
     loads = []
-    for n, (src, dst) in enumerate(((w_in, W2.at[yl]), (gate_in, gate), (up_in, up), (cot_in, cot))):
+    for n, (src, dst) in enumerate(((cot_in, cot), (gate_in, gate), (up_in, up), (w_in, W2.at[yl]))):
         loads.append(pltpu.make_async_copy(src, dst, in_sem.at[n]))
         loads[-1].start()
 
@@ -122,13 +122,9 @@
         HT[x, rows, :] = (g * jax.nn.sigmoid(g) * up[rows, :].astype(F32)).astype(BF)
         return 0
 
-    loads[3].wait()
+    loads[0].wait()
     for r in range(0, HALF, 128):
         OWN[:, r : r + 128] = cot[r : r + 128, :].astype(F32).T.astype(BF)
-    loads[0].wait()
-    loads[1].wait()
-    loads[2].wait()
-    lax.fori_loop(0, 29, make_hidden, 0)
 
     pl.semaphore_wait(barrier, len(greeted))
     cp = Copies(send_sem, recv_sem)
@@ -145,12 +141,17 @@
         at = pl.ds(k * RC, RC)
         t1.append(cp.put_or_keep(t1_keep, OWN.at[at], ZM.at[0, at], T1)[1])
 
+    loads[1].wait()
+    loads[2].wait()
+    lax.fori_loop(0, 29, make_hidden, 0)
+    a0, a1 = pl.ds(0, 240), pl.ds(FF - 240, 240)
+    s1p, s1m = [share(HT.at[x, a0], X(1))], [share(HT.at[x, a1], X(-1))]
+    loads[3].wait()
+
     def send_w(start, size):
         return share(W2.at[yl, :, pl.ds(start, size)], YL)
 
     ws = [send_w(0, 128)]
-    a0, a1 = pl.ds(0, 240), pl.ds(FF - 240, 240)
-    s1p, s1m = [share(HT.at[x, a0], X(1))], [share(HT.at[x, a1], X(-1))]
 
     def turn(s, n):
         WT[s, pl.ds(n * 256, 256), :] = W2[s, :, pl.ds(n * 256, 256)].astype(F32).T.astype(BF)
@@ -213,7 +214,11 @@
     for n in range(4):
         turn(yl, n)
 
-    def make_layer(s, k, first, step, count):
+    lx = {}
+
+    def make_layer(other, k, first, step, count):
+        s = 1 - yl if other else yl
+
         def part(n, _):
             g, cols = (x + first + step * (n // 2)) % 4, pl.ds(pl.multiple_of((n % 2) * 256, 256), 256)
             there = pl.ds(pl.multiple_of((1 - c) * HALF + k * RL, RL), RL)
@@ -225,16 +230,17 @@
 
         lax.fori_loop(0, 2 * count, part, 0)
 
-    def cross_layer(s, k):
-        return cp.put(LS.at[s, k], LX.at[s, k], CORE)
+        for n in range(count):
+            g = (x + first + step * n) % 4
+            lx.setdefault((other, k), []).append(cp.put(LS.at[s, k, g], LX.at[s, k, g], CORE))
 
     cross(0, 0)
     cross(0, 1)
     s1p[0].wait_recv()
     s1m[0].wait_recv()
     s2 = [share(HT.at[tok(-1), a0], X(1)), share(HT.at[tok(1), a1], X(-1))]
-    make_layer(yl, 0, 0, 1, 1)
-    make_layer(yl, 1, 0, 1, 1)
+    make_layer(False, 0, 0, 1, 1)
+    make_layer(False, 1, 0, 1, 1)
     s1p[1].wait_recv()
     s1m[1].wait_recv()
     s2 += [share(HT.at[tok(-1), a0b], X(1)), share(HT.at[tok(1), a1b], X(-1))]
@@ -244,25 +250,26 @@
             near[b, k][0].wait_recv()
             near[b, k][1].wait_recv()
             far[b, k] = forward(b, k)
+        if k == 1:
+            s1p[2].wait_recv()
+            s1m[2].wait_recv()
+            make_layer(False, 0, 1, 2, 2)
+        if k == 2:
+            make_layer(False, 1, 1, 2, 2)
+            ws[0].wait_recv()
+            ws[1].wait_recv()
+            turn(1 - yl, 0)
     for b in range(2):
         cross(1, b)
         cross(-1, b)
-    s1p[2].wait_recv()
-    s1m[2].wait_recv()
-    make_layer(yl, 0, 1, 2, 2)
-    make_layer(yl, 1, 1, 2, 2)
-    for w in ws[:3]:
-        w.wait_recv()
-    turn(1 - yl, 0)
+    ws[2].wait_recv()
     turn(1 - yl, 2)
-    make_layer(1 - yl, 0, 0, 1, 2)
-    make_layer(1 - yl, 0, 3, 1, 1)
+    make_layer(True, 0, 0, 1, 2)
+    make_layer(True, 0, 3, 1, 1)
     for f in s2:
         f.wait_recv()
-    make_layer(yl, 0, 2, 1, 1)
-    lx = {0: cross_layer(yl, 0)}
-    make_layer(1 - yl, 0, 2, 1, 1)
-    lx[1] = cross_layer(1 - yl, 0)
+    make_layer(False, 0, 2, 1, 1)
+    make_layer(True, 0, 2, 1, 1)
     for b in range(2):
         for k in range(C):
             far[b, k][0].wait_recv()
@@ -336,41 +343,42 @@
         ).astype(BF)
         cp.put_or_keep(token == x, LO.at[s, k, token], BX.at[x1, k], owner(b), (back_at[k] + b, back_at[k] + x1))
 
-    lx[0].wait_recv()
-    lx[1].wait_recv()
+    for other in range(2):
+        for f in lx[other, 0]:
+            f.wait_recv()
     begin(0)
     for f in t5:
         f.wait_recv()
     partner_sum(0)
     send_sum(0)
-    make_layer(yl, 1, 2, 1, 1)
-    lx[2] = cross_layer(yl, 1)
+    make_layer(False, 1, 2, 1, 1)
     ws[3].wait_recv()
     ws[4].wait_recv()
-    turn(1 - yl, 1)
-    turn(1 - yl, 3)
-    make_layer(1 - yl, 1, 0, 1, 4)
-    lx[3] = cross_layer(1 - yl, 1)
-    relay(0, 0)
-    relay(1, 0)
     make_grad(tok(2))
     g2a = cp.put(G.at[tok(2), low], RAB.at[low], X(1))
     g2b = cp.put(G.at[tok(2), high], RAB.at[high], X(-1))
+    relay(0, 0)
+    turn(1 - yl, 1)
+    turn(1 - yl, 3)
+    make_layer(True, 1, 0, 1, 2)
+    relay(1, 0)
+    make_layer(True, 1, 2, 1, 2)
     partner_sum(1)
     send_sum(1)
-    lx[2].wait_recv()
-    lx[3].wait_recv()
+    for other in range(2):
+        for f in lx[other, 1]:
+            f.wait_recv()
     begin(1)
     for k in range(CL):
         pair(0, 0, k)
         pair(0, 1, k)
     up_one, down_one = tok(1), tok(-1)
     make_grad(up_one)
+    send_back(0, 0)
+    g5 = [cp.put(G.at[up_one, high], RO.at[0, high], X(1))]
     partner_sum(2)
     send_sum(2)
-    send_back(0, 0)
     send_back(1, 0)
-    g5 = [cp.put(G.at[up_one, high], RO.at[0, high], X(1))]
     make_grad(down_one)
     g5.append(cp.put(G.at[down_one, low], RO.at[1, low], X(-1)))
     relay(0, 1)
@@ -422,6 +430,13 @@
     send_sum(3, CUT, FF - CUT)
     home(0)
     own_sum(1)
+    weight_sum(yl, 2)
+    gd[2][0].wait_recv()
+    outs[0].wait()
+    gd_stage[0] = (acc[...] + GDR[2].astype(F32)).astype(BF)
+    third = pltpu.make_async_copy(gd_stage.at[0], gd_out.at[:, pl.ds(512, 256)], out_sem.at[2])
+    third.start()
+    weight_sum(yl, 3)
     home(1)
 
     for f in g5:
@@ -443,13 +458,13 @@
         copy = pltpu.make_async_copy(stage, out, out_sem.at[5 + n])
         copy.start()
         outs.append(copy)
-    weight_sum(yl, 2)
-    gd[2][0].wait_recv()
-    outs[0].wait()
-    gd_stage[0] = (acc[...] + GDR[2].astype(F32)).astype(BF)
-    third = pltpu.make_async_copy(gd_stage.at[0], gd_out.at[:, pl.ds(512, 256)], out_sem.at[2])
-    third.start()
-    weight_sum(yl, 3)
+    gd[3][0].wait_recv()
+    gd[3][1].wait_recv()
+    outs[1].wait()
+    gd_stage[1] = (acc[...] + GDR[3].astype(F32)).astype(BF)
+    fourth = pltpu.make_async_copy(gd_stage.at[1], gd_out.at[:, pl.ds(768, 256)], out_sem.at[3])
+    fourth.start()
+    cp.finish()
 
     for k in range(CL):
         at = pl.ds(k * RL, RL)
@@ -459,12 +474,6 @@
     lay = pltpu.make_async_copy(lay_stage, lay_out, out_sem.at[4])
     lay.start()
     cp.finish()
-    outs[1].wait()
-    gd[3][0].wait_recv()
-    gd[3][1].wait_recv()
-    gd_stage[1] = (acc[...] + GDR[3].astype(F32)).astype(BF)
-    fourth = pltpu.make_async_copy(gd_stage.at[1], gd_out.at[:, pl.ds(768, 256)], out_sem.at[3])
-    fourth.start()
     for copy in (outs[2], outs[3], third, lay, fourth):
         copy.wait()
 

time: 132 us -> 127 us (0.962); the launches traced: 132 us -> 125 us
  Pallas kernels: 131 us -> 124 us
    pallas_call x1, Pallas kernels: 127 us -> 121 us  [shards(): pl.pallas_call(kernel, out_shape=shapes, in_specs=[anywhere] * 4, out_spe...]
where the time goes in v6:
time: 127 us; the launch traced here: 125 us
  Pallas kernels  124 us (98%)
    pallas_call x1, Pallas kernels, shards(): pl.pallas_call(kernel, out_shape=shapes, in_specs=[anywhere] * 4, out_spe...  121 us
    pallas_call x1, Pallas kernels, shards(): pl.pallas_call(place_outputs, out_shape=shapes, in_specs=[anywhere] * 4,...  3.57 us

profile of v6, /device:TPU:1, one launch (start us, length us, event | category | flops | bytes accessed | tf_op | source)
XLA Modules:
  0.0 124.9 jit_solution(12227646540931782304)
XLA Ops:
  0.6 120.6 %shard_map.75 = (bf16[512,512]{1,0:T(8,128)(2,1)}, bf16[928,512]{1,0:T(8,128)(2,1)}, bf16[928,512]{1,0:T(8,128)(2,1)}, bf16[928,1024]{1,0:T(8,128)(2,1)}) custom-call(bf16[928,512]{1,0:T(8,128)(2,1)} %bitcast.4, bf16[928,512]{1,0:T(8,128)(2,1)} %bitcast.5, bf16[928,1024]{1,0:T(8,128)(2,1)} %w_in.1, bf16[512,512]{1,0:T(8,128)(2,1)} %cot_in.1), custom_call_target="tpu_custom_call" | custom-call | flops 23353884672 | bytes 16777216 | tf_op jit(solution)/shard_map/pallas_call | solution.py:509
  121.2 3.6 %shard_map.76 = (bf16[512,512]{1,0:T(8,128)(2,1)}, bf16[928,512]{1,0:T(8,128)(2,1)}, bf16[928,512]{1,0:T(8,128)(2,1)}, bf16[928,1024]{1,0:T(8,128)(2,1)}) custom-call(bf16[512,512]{1,0:T(8,128)(2,1)} %get-tuple-element.12.refs_0_, bf16[928,512]{1,0:T(8,128)(2,1)} %get-tuple-element.13.refs_1_, bf16[928,512]{1,0:T(8,128)(2,1)} %get-tuple-element.14.refs_2_, ...), custom_call_target="tpu_custom_call" | custom-call | tf_op jit(solution)/shard_map/pallas_call | solution.py:553

commit v7 on v6

--- a/solution.py
+++ b/solution.py
@@ -145,6 +145,7 @@
     loads[2].wait()
     lax.fori_loop(0, 29, make_hidden, 0)
     a0, a1 = pl.ds(0, 240), pl.ds(FF - 240, 240)
+    a0b, a1b = pl.ds(240, CUT - 240), pl.ds(CUT, FF - 240 - CUT)
     s1p, s1m = [share(HT.at[x, a0], X(1))], [share(HT.at[x, a1], X(-1))]
     loads[3].wait()
 
@@ -198,12 +199,12 @@
         if k > 0:
             t3[k - 1].wait_recv()
             send_t2(1, k - 1)
+        if k == 1:
+            s1p.append(share(HT.at[x, a0b], X(1)))
+            s1m.append(share(HT.at[x, a1b], X(-1)))
     owned(0)
     t3[-1].wait_recv()
     send_t2(1, C - 1)
-    a0b, a1b = pl.ds(240, CUT - 240), pl.ds(CUT, FF - 240 - CUT)
-    s1p.append(share(HT.at[x, a0b], X(1)))
-    s1m.append(share(HT.at[x, a1b], X(-1)))
     for start, size in ((128, 128), (512, 256), (256, 256), (768, 256)):
         ws.append(send_w(start, size))
     s1p.append(share(HT.at[x, high], X(1)))
@@ -332,7 +333,8 @@
             sent.append(cp.put(LO.at[s, k, token], LD.at[b, side, k], Z(dz)))
         directs[b, k] = sent
 
-    back_at = [cp.ids(2) for _ in range(CL)]
+    PARTS = ((0, 0, RL), (1, 0, HL), (1, HL, HL))
+    back_at = [cp.ids(2) for _ in PARTS]
 
     def send_back(b, k):
         token, s = place(0, b)
@@ -341,7 +343,11 @@
         LO[s, k, token] = (
             LO[s, k, token].astype(F32) + LD[b, 0, k].astype(F32) + LD[b, 1, k].astype(F32)
         ).astype(BF)
-        cp.put_or_keep(token == x, LO.at[s, k, token], BX.at[x1, k], owner(b), (back_at[k] + b, back_at[k] + x1))
+        for p, (piece, start, size) in enumerate(PARTS):
+            if piece == k:
+                at = pl.ds(start, size)
+                sems = (back_at[p] + b, back_at[p] + x1)
+                cp.put_or_keep(token == x, LO.at[s, k, token, at], BX.at[x1, k, at], owner(b), sems)
 
     for other in range(2):
         for f in lx[other, 0]:
@@ -387,10 +393,12 @@
 
     ly = []
 
-    def meet(k):
+    def meet(p):
+        k, start, size = PARTS[p]
+        at = pl.ds(start, size)
         for r in range(2):
-            cp.landed(2 * r + hz == x, LO.at[0, 0, 0], BX.at[r, k], back_at[k] + r, owner(r))
-        ly.append(cp.put(BX.at[1 - yh, k], BY.at[k], YH))
+            cp.landed(2 * r + hz == x, LO.at[0, 0, 0, at], BX.at[r, k, at], back_at[p] + r, owner(r))
+        ly.append(cp.put(BX.at[1 - yh, k, at], BY.at[k, at], YH))
 
     meet(0)
     send_sum(3, 0, CUT)
@@ -406,10 +414,11 @@
 
     sw = []
 
-    def home(k):
-        ly[k].wait_recv()
-        at = pl.ds(k * RL, RL)
-        FIN[at] = (BX[yh, k].astype(F32) + BY[k].astype(F32)).astype(BF)
+    def home(p):
+        k, start, size = PARTS[p]
+        ly[p].wait_recv()
+        part, at = pl.ds(start, size), pl.ds(k * RL + start, size)
+        FIN[at] = (BX[yh, k, part].astype(F32) + BY[k, part].astype(F32)).astype(BF)
         sw.append(cp.put_or_keep(t1_keep, FIN.at[at], SWP.at[at], T1S)[1])
 
     outs = []
@@ -427,6 +436,7 @@
 
     own_sum(0)
     meet(1)
+    meet(2)
     send_sum(3, CUT, FF - CUT)
     home(0)
     own_sum(1)
@@ -436,8 +446,9 @@
     gd_stage[0] = (acc[...] + GDR[2].astype(F32)).astype(BF)
     third = pltpu.make_async_copy(gd_stage.at[0], gd_out.at[:, pl.ds(512, 256)], out_sem.at[2])
     third.start()
+    home(1)
     weight_sum(yl, 3)
-    home(1)
+    home(2)
 
     for f in g5:
         f.wait_recv()
@@ -458,6 +469,21 @@
         copy = pltpu.make_async_copy(stage, out, out_sem.at[5 + n])
         copy.start()
         outs.append(copy)
+    lays = []
+
+    def settle(p):
+        k, start, size = PARTS[p]
+        at = pl.ds(k * RL + start, size)
+        cp.landed(t1_keep, FIN.at[at], SWP.at[at], sw[p], T1S)
+        for first in range(k * RL + start, k * RL + start + size, 128):
+            n, at = first // 128, pl.ds(first, 128)
+            for r in range(0, TOK, 128):
+                lay_stage[n, r : r + 128, :] = SWP[at, r : r + 128].astype(F32).T.astype(BF)
+            lays.append(pltpu.make_async_copy(lay_stage.at[n], lay_out.at[:, at], out_sem.at[7 + n]))
+            lays[n].start()
+
+    settle(0)
+    settle(1)
     gd[3][0].wait_recv()
     gd[3][1].wait_recv()
     outs[1].wait()
@@ -466,15 +492,8 @@
     fourth.start()
     cp.finish()
 
-    for k in range(CL):
-        at = pl.ds(k * RL, RL)
-        cp.landed(t1_keep, FIN.at[at], SWP.at[at], sw[k], T1S)
-        for r in range(0, TOK, 128):
-            lay_stage[r : r + 128, k * RL : (k + 1) * RL] = SWP[at, r : r + 128].astype(F32).T.astype(BF)
-    lay = pltpu.make_async_copy(lay_stage, lay_out, out_sem.at[4])
-    lay.start()
-    cp.finish()
-    for copy in (outs[2], outs[3], third, lay, fourth):
+    settle(2)
+    for copy in (outs[2], outs[3], third, fourth, *lays):
         copy.wait()
 
 
@@ -537,13 +556,13 @@
             pltpu.VMEM((4, FF, 256), BF),
             pltpu.VMEM((4, FF, 256), BF),
             pltpu.VMEM((2, FF, 256), BF),
-            pltpu.VMEM((TOK, HALF), BF),
+            pltpu.VMEM((HALF // 128, TOK, 128), BF),
             pltpu.VMEM((FF, TOK), BF),
             pltpu.VMEM((FF, TOK), BF),
             pltpu.SemaphoreType.DMA((n_copies,)),
             pltpu.SemaphoreType.DMA((n_copies,)),
             pltpu.SemaphoreType.DMA((4,)),
-            pltpu.SemaphoreType.DMA((7,)),
+            pltpu.SemaphoreType.DMA((7 + HALF // 128,)),
         ],
         compiler_params=pltpu.CompilerParams(
             collective_id=0, has_side_effects=True, vmem_limit_bytes=64 * 2**20

time: 127 us -> 125 us (0.984); the launches traced: 125 us -> 125 us
  no operation moved by 1% of the time
where the time goes in v7:
time: 125 us
  Pallas kernels  124 us (99%)
    pallas_call x1, Pallas kernels, shards(): pl.pallas_call(kernel, out_shape=shapes, in_specs=[anywhere] * 4, out_spe...  121 us
    pallas_call x1, Pallas kernels, shards(): pl.pallas_call(place_outputs, out_shape=shapes, in_specs=[anywhere] * 4,...  3.57 us

profile of v7, /device:TPU:1, one launch (start us, length us, event | category | flops | bytes accessed | tf_op | source)
XLA Modules:
  0.0 125.2 jit_solution(15273285694257939125)
XLA Ops:
  0.6 120.8 %shard_map.75 = (bf16[512,512]{1,0:T(8,128)(2,1)}, bf16[928,512]{1,0:T(8,128)(2,1)}, bf16[928,512]{1,0:T(8,128)(2,1)}, bf16[928,1024]{1,0:T(8,128)(2,1)}) custom-call(bf16[928,512]{1,0:T(8,128)(2,1)} %bitcast.4, bf16[928,512]{1,0:T(8,128)(2,1)} %bitcast.5, bf16[928,1024]{1,0:T(8,128)(2,1)} %w_in.1, bf16[512,512]{1,0:T(8,128)(2,1)} %cot_in.1), custom_call_target="tpu_custom_call" | custom-call | flops 23353884672 | bytes 16777216 | tf_op jit(solution)/shard_map/pallas_call | solution.py:528
  121.4 3.6 %shard_map.76 = (bf16[512,512]{1,0:T(8,128)(2,1)}, bf16[928,512]{1,0:T(8,128)(2,1)}, bf16[928,512]{1,0:T(8,128)(2,1)}, bf16[928,1024]{1,0:T(8,128)(2,1)}) custom-call(bf16[512,512]{1,0:T(8,128)(2,1)} %get-tuple-element.12.refs_0_, bf16[928,512]{1,0:T(8,128)(2,1)} %get-tuple-element.13.refs_1_, bf16[928,512]{1,0:T(8,128)(2,1)} %get-tuple-element.14.refs_2_, ...), custom_call_target="tpu_custom_call" | custom-call | tf_op jit(solution)/shard_map/pallas_call | solution.py:572

commit v8 on v7

--- a/solution.py
+++ b/solution.py
@@ -434,6 +434,19 @@
         copy.start()
         outs.append(copy)
 
+    lays = []
+
+    def settle(p):
+        k, start, size = PARTS[p]
+        at = pl.ds(k * RL + start, size)
+        cp.landed(t1_keep, FIN.at[at], SWP.at[at], sw[p], T1S)
+        for first in range(k * RL + start, k * RL + start + size, 128):
+            n, at = first // 128, pl.ds(first, 128)
+            for r in range(0, TOK, 128):
+                lay_stage[n, r : r + 128, :] = SWP[at, r : r + 128].astype(F32).T.astype(BF)
+            lays.append(pltpu.make_async_copy(lay_stage.at[n], lay_out.at[:, at], out_sem.at[7 + n]))
+            lays[n].start()
+
     own_sum(0)
     meet(1)
     meet(2)
@@ -448,6 +461,7 @@
     third.start()
     home(1)
     weight_sum(yl, 3)
+    settle(0)
     home(2)
 
     for f in g5:
@@ -469,20 +483,6 @@
         copy = pltpu.make_async_copy(stage, out, out_sem.at[5 + n])
         copy.start()
         outs.append(copy)
-    lays = []
-
-    def settle(p):
-        k, start, size = PARTS[p]
-        at = pl.ds(k * RL + start, size)
-        cp.landed(t1_keep, FIN.at[at], SWP.at[at], sw[p], T1S)
-        for first in range(k * RL + start, k * RL + start + size, 128):
-            n, at = first // 128, pl.ds(first, 128)
-            for r in range(0, TOK, 128):
-                lay_stage[n, r : r + 128, :] = SWP[at, r : r + 128].astype(F32).T.astype(BF)
-            lays.append(pltpu.make_async_copy(lay_stage.at[n], lay_out.at[:, at], out_sem.at[7 + n]))
-            lays[n].start()
-
-    settle(0)
     settle(1)
     gd[3][0].wait_recv()
     gd[3][1].wait_recv()
@@ -501,14 +501,15 @@
     sources, results, stages, sems = refs[:4], refs[4:8], refs[8:12], refs[12]
     arrive, leave = [], []
     for n in (0, 3, 1, 2):
-        rows = sources[n].shape[0] // 2
-        for part in range(2):
-            at, k = pl.ds(part * rows, rows), len(arrive)
+        rows = sources[n].shape[0]
+        for part in range(4):
+            start = part * rows // 64 * 16
+            at, k = pl.ds(start, (part + 1) * rows // 64 * 16 - start), len(arrive)
             arrive.append(pltpu.make_async_copy(sources[n].at[at], stages[n].at[at], sems.at[k]))
-            leave.append(pltpu.make_async_copy(stages[n].at[at], results[n].at[at], sems.at[8 + k]))
+            leave.append(pltpu.make_async_copy(stages[n].at[at], results[n].at[at], sems.at[16 + k]))
     for copy in arrive:
         copy.start()
-    for k in range(8):
+    for k in range(16):
         arrive[k].wait()
         leave[k].start()
     for copy in leave:
@@ -574,7 +575,7 @@
         out_shape=shapes,
         in_specs=[anywhere] * 4,
         out_specs=[anywhere] * 4,
-        scratch_shapes=[pltpu.VMEM(shape.shape, BF) for shape in shapes] + [pltpu.SemaphoreType.DMA((16,))],
+        scratch_shapes=[pltpu.VMEM(shape.shape, BF) for shape in shapes] + [pltpu.SemaphoreType.DMA((32,))],
         compiler_params=pltpu.CompilerParams(vmem_limit_bytes=64 * 2**20),
     )(*results)
     return layer_out, grad_gate.T, grad_up.T, grad_down

time: 125 us -> 126 us (level)
  no operation moved by 1% of the time
where the time goes in v8:
time: 126 us
  Pallas kernels  125 us (99%)
    pallas_call x1, Pallas kernels, shards(): pl.pallas_call(kernel, out_shape=shapes, in_specs=[anywhere] * 4, out_spe...  121 us
    pallas_call x1, Pallas kernels, shards(): pl.pallas_call(place_outputs, out_shape=shapes, in_specs=[anywhere] * 4,...  4.15 us

profile of v8, /device:TPU:1, one launch (start us, length us, event | category | flops | bytes accessed | tf_op | source)
XLA Modules:
  0.0 125.7 jit_solution(9797010559623119171)
XLA Ops:
  0.6 120.8 %shard_map.75 = (bf16[512,512]{1,0:T(8,128)(2,1)}, bf16[928,512]{1,0:T(8,128)(2,1)}, bf16[928,512]{1,0:T(8,128)(2,1)}, bf16[928,1024]{1,0:T(8,128)(2,1)}) custom-call(bf16[928,512]{1,0:T(8,128)(2,1)} %bitcast.4, bf16[928,512]{1,0:T(8,128)(2,1)} %bitcast.5, bf16[928,1024]{1,0:T(8,128)(2,1)} %w_in.1, bf16[512,512]{1,0:T(8,128)(2,1)} %cot_in.1), custom_call_target="tpu_custom_call" | custom-call | flops 23353884672 | bytes 16777216 | tf_op jit(solution)/shard_map/pallas_call | solution.py:529
  121.4 4.2 %shard_map.76 = (bf16[512,512]{1,0:T(8,128)(2,1)}, bf16[928,512]{1,0:T(8,128)(2,1)}, bf16[928,512]{1,0:T(8,128)(2,1)}, bf16[928,1024]{1,0:T(8,128)(2,1)}) custom-call(bf16[512,512]{1,0:T(8,128)(2,1)} %get-tuple-element.12.refs_0_, bf16[928,512]{1,0:T(8,128)(2,1)} %get-tuple-element.13.refs_1_, bf16[928,512]{1,0:T(8,128)(2,1)} %get-tuple-element.14.refs_2_, ...), custom_call_target="tpu_custom_call" | custom-call | tf_op jit(solution)/shard_map/pallas_call | solution.py:573
